TPU v7x, 32 devices: a whole 2x2x4 slice. The times are simulated.
32 devices in a mesh: rows: 8 (over z, x), rep: 4 (over y, core).
Axes of the slice: x: 2, y: 2, z: 4, core: 2. Of those that a mesh axis runs over, the one named last changes fastest.
Arguments:
- feats: bfloat16 [4, 2048, 512], P('rep', 'rows'), may hold values from -24 to 24
- grad_out: bfloat16 [4, 2048, 512], P('rep', 'rows'), may hold values from -6 to 6
- qkv_weight: bfloat16 [512, 1536], P('rows'), may hold values from -0.25 to 0.25
- proj_weight: bfloat16 [512, 512], P('rows'), may hold values from -0.25 to 0.25
- to_hilbert: int32 [4, 64], P('rep', 'rows'), may hold values from 0 to 63, as said below
- to_zorder: int32 [4, 64], P('rep', 'rows'), may hold values from 0 to 63, as said below
Outputs:
- grad_feats: bfloat16 [4, 2048, 512], P('rep', 'rows')
- qkv_grad: float32 [512, 1536], P('rows')
- proj_grad: float32 [512, 512], P('rows')
Inputs may be any that keep to these rules, and one draw needn't show every extreme that they name: to_hilbert[s] is a permutation of the blocks of scene s and to_zorder[s] its inverse; of the 8 Z-order blocks of one device, at most 2 have Hilbert positions on any one device, and exactly 2 for some pair of devices in every scene. `to_zorder`: the inverse of to_hilbert in every scene.
All inputs are finite; a program needn't handle non-finite values.
Results may differ from a plain program's by a relative error of at most 0.015.
The roundings to bfloat16 on the way count: a program that leaves them out, or rounds other values in their place, can miss the bound.
Values may be sent and summed in bfloat16 or wider, within the bound.
A program may use at most 64 MiB of HBM per device.

v0:
```python
import jax
import jax.numpy as jnp
from jax import lax
from jax.sharding import PartitionSpec as P

HEADS = 8
CAP = 2


def from_partner(block, axis, apart):
    count = lax.axis_size(axis)
    route = []
    for low in range(count):
        high = low | 1 << apart
        if high != low and high < count:
            route += [(low, high), (high, low)]
    return lax.ppermute(block, axis, route)


def move_blocks(outgoing):
    return lax.all_to_all(outgoing, "rows", split_axis=0, concat_axis=0, tiled=True)


def rank_within(order_keys, owners):
    same_owner = owners[None, :] == owners[:, None]
    earlier = order_keys[None, :] < order_keys[:, None]
    return jnp.sum(jnp.logical_and(same_owner, earlier).astype(jnp.int32), axis=1)


def contract_rows(left, right):
    return lax.dot_general(
        left, right, (((0,), (0,)), ((), ())), preferred_element_type=jnp.float32
    )


def contract_cols(left, right):
    return lax.dot_general(
        left, right, (((1,), (1,)), ((), ())), preferred_element_type=jnp.float32
    )


def per_device(feats, grad_out, qkv_weight, proj_weight, to_hilbert, to_zorder):
    peer_count = lax.axis_size("rows")
    feature = feats[0]
    rows_dev, channels = feature.shape
    head_size = channels // HEADS
    scale = head_size ** (-0.5)
    blocks_dev = to_hilbert.shape[1]
    slot_count = peer_count * CAP
    w_qkv, w_proj = (
        lax.all_gather(qkv_weight, "rows", axis=0, tiled=True),
        lax.all_gather(proj_weight, "rows", axis=0, tiled=True),
    )
    forward_list = to_hilbert[0]
    inverse_list = to_zorder[0]
    local_ids = jnp.arange(blocks_dev, dtype=jnp.int32)
    slot_ids = jnp.arange(slot_count, dtype=jnp.int32)
    target_dev = forward_list // blocks_dev
    send_slot = target_dev * CAP + rank_within(local_ids, target_dev)
    send_table = (send_slot[None, :] == slot_ids[:, None]).astype(jnp.bfloat16)
    source_dev = inverse_list // blocks_dev
    recv_slot = source_dev * CAP + rank_within(inverse_list, source_dev)
    recv_table = (recv_slot[:, None] == slot_ids[None, :]).astype(jnp.bfloat16)
    zblocks = grad_out[0].reshape(blocks_dev, -1)
    outgoing = jnp.dot(send_table, zblocks, preferred_element_type=jnp.float32).astype(jnp.bfloat16)
    arrived = move_blocks(outgoing.reshape(peer_count, CAP, -1)).reshape(slot_count, -1)
    grad_hil = jnp.dot(recv_table, arrived, preferred_element_type=jnp.float32).astype(jnp.bfloat16)
    grad_hil = grad_hil.reshape(rows_dev, channels)
    qkv = jnp.dot(feature, w_qkv, preferred_element_type=jnp.float32).astype(jnp.bfloat16)
    query = qkv[:, :channels]
    keyval = qkv[:, channels:]
    grad_attn = contract_cols(grad_hil, w_proj).astype(jnp.bfloat16)
    other_kv = from_partner(keyval, "rows", 0)
    keys_all = jnp.concatenate([keyval[:, :channels], other_kv[:, :channels]], axis=0)
    values_all = jnp.concatenate([keyval[:, channels:], other_kv[:, channels:]], axis=0)
    attn_parts, dq_parts, dk_parts, dv_parts = ([], [], [], [])
    for head_index in range(HEADS):
        lo_col = head_index * head_size
        q_head = query[:, lo_col : lo_col + head_size]
        k_head = keys_all[:, lo_col : lo_col + head_size]
        v_head = values_all[:, lo_col : lo_col + head_size]
        g_head = grad_attn[:, lo_col : lo_col + head_size]
        score = contract_cols(q_head, k_head) * scale
        row_max = jnp.max(score, axis=1, keepdims=True)
        raised = jnp.exp(score - row_max)
        row_sum = jnp.sum(raised, axis=1, keepdims=True)
        probs = raised / row_sum
        probs_b = probs.astype(jnp.bfloat16)
        attn_parts.append(
            jnp.dot(probs_b, v_head, preferred_element_type=jnp.float32).astype(jnp.bfloat16)
        )
        dprob = contract_cols(g_head, v_head)
        delta = jnp.sum(probs * dprob, axis=1, keepdims=True)
        dscore = (probs * (dprob - delta) * scale).astype(jnp.bfloat16)
        dq_parts.append(jnp.dot(dscore, k_head, preferred_element_type=jnp.float32))
        dk_parts.append(contract_rows(dscore, q_head))
        dv_parts.append(contract_rows(probs_b, g_head))
    grad_q = jnp.concatenate(dq_parts, axis=1)
    grad_k = jnp.concatenate(dk_parts, axis=1)
    grad_v = jnp.concatenate(dv_parts, axis=1)
    other_k, other_v = (
        from_partner(grad_k[rows_dev:].astype(jnp.bfloat16), "rows", 0).astype(jnp.float32),
        from_partner(grad_v[rows_dev:].astype(jnp.bfloat16), "rows", 0).astype(jnp.float32),
    )
    grad_k = grad_k[:rows_dev] + other_k
    grad_v = grad_v[:rows_dev] + other_v
    grad_qkv = jnp.concatenate([grad_q, grad_k, grad_v], axis=1).astype(jnp.bfloat16)
    attn = jnp.concatenate(attn_parts, axis=1)
    grad_hfeat = contract_cols(grad_qkv, w_qkv).astype(jnp.bfloat16)
    hblocks = grad_hfeat.reshape(blocks_dev, -1)
    going_back = contract_rows(recv_table, hblocks).astype(jnp.bfloat16)
    returned = move_blocks(going_back.reshape(peer_count, CAP, -1)).reshape(slot_count, -1)
    grad_z = contract_rows(send_table, returned).astype(jnp.bfloat16).reshape(rows_dev, channels)
    share = channels // peer_count
    term = jnp.concatenate(
        [contract_rows(feature, grad_qkv), contract_rows(attn, grad_hil)], axis=1
    )
    total = lax.psum(term, ("rows", "rep"))
    owned = lax.dynamic_slice_in_dim(total, lax.axis_index("rows") * share, share, 0)
    return (grad_z[None], owned[:, : 3 * channels], owned[:, 3 * channels :])


def solution(mesh):
    placed = (
        P("rep", "rows", None),
        P("rep", "rows", None),
        P("rows", None),
        P("rows", None),
        P("rep", "rows"),
        P("rep", "rows"),
    )
    return jax.shard_map(
        per_device,
        mesh=mesh,
        in_specs=placed,
        out_specs=(P("rep", "rows", None), P("rows", None), P("rows", None)),
        check_vma=False,
    )
```

profile of v0, /device:TPU:0, one launch (start us, length us, event | category | flops | bytes accessed | tf_op | source)
XLA Modules:
  0.0 312.3 jit_solution(13380712824804140087)
XLA Ops:
  7.9 1.1 reshape_squeeze.3
  11.5 1.1 reshape.119
  12.6 7.3 %all-to-all-start = ((bf16[8,2,16384]{2,1,0:T(2,128)(2,1)}), bf16[8,2,16384]{2,1,0:T(2,128)(2,1)S(1)}, u32[]{:S(2)}, u32[]{:S(2)}) async-start(bf16[8,2,16384]{2,1,0:T(2,128)(2,1)} %reshape.119), calls=%async_computation | async-start | bytes 1048576 | tf_op jit(solution)/shard_map/all_to_all | solution.py:21
  20.2 45.5 %all_gather.7 = bf16[512,512]{1,0:T(8,128)(2,1)S(1)} all-gather(bf16[64,512]{1,0:T(8,128)(2,1)S(1)} %copy-done.25), channel_id=1, replica_groups=mesh['rows'=8,'rep'=4] {'rows'}, dimensions={0}, use_global_device_ids=true | all-gather | bytes 589824 | tf_op jit(solution)/shard_map/all_gather | solution.py:52
  65.9 1.4 all-gather.2.cloned.1.call-done
  67.3 2.0 convolution_convert_fusion.4
  69.3 0.9 slice.187
  70.2 2.2 collective-permute-start
  73.2 11.3 %collective-permute-done = bf16[256,1024]{1,0:T(8,128)(2,1)S(1)} collective-permute-done((bf16[256,1024]{1,0:T(8,128)(2,1)}, bf16[256,1024]{1,0:T(8,128)(2,1)S(1)}, u32[]{:S(2)}, u32[]{:S(2)}) %collective-permute-start) | collective-permute-done | bytes 524320 | tf_op jit(solution)/shard_map/ppermute | solution.py:17
  85.8 0.9 convolution_convert_fusion.7
  86.7 1.6 multiply_reduce_fusion
  88.5 0.9 convolution_convert_fusion.14
  90.1 1.2 fusion.154
  91.6 1.0 convolution_convert_fusion.13
  92.6 2.5 multiply_reduce_fusion.6
  95.1 1.2 fusion.155
  96.5 0.9 convolution_convert_fusion.12
  97.4 2.4 multiply_reduce_fusion.5
  99.8 1.2 fusion.156
  101.3 1.0 convolution_convert_fusion.11
  102.3 2.5 multiply_reduce_fusion.4
  104.8 1.2 fusion.157
  106.2 0.9 convolution_convert_fusion.10
  107.1 2.4 multiply_reduce_fusion.3
  109.5 1.2 fusion.158
  111.0 1.0 convolution_convert_fusion.9
  112.0 2.5 multiply_reduce_fusion.2
  114.5 1.1 fusion.159
  115.9 0.9 convolution_convert_fusion.8
  116.8 2.5 multiply_reduce_fusion.1
  123.5 1.0 copy-done.15
  125.2 1.7 collective-permute-start.2
  127.0 1.9 concatenate.27
  129.0 1.4 fusion.161
  130.4 1.4 multiply_convert_fusion.6
  131.9 0.9 fusion.6
  135.3 1.0 fusion.4
  141.2 6.2 %collective-permute-done.1 = bf16[256,512]{0,1:T(8,128)(2,1)S(1)} collective-permute-done((bf16[256,512]{0,1:T(8,128)(2,1)S(1)}, bf16[256,512]{0,1:T(8,128)(2,1)S(1)}, u32[]{:S(2)}, u32[]{:S(2)}) %collective-permute-start.1) | collective-permute-done | bytes 262176 | tf_op jit(solution)/shard_map/ppermute | solution.py:17
  147.5 1.0 fusion.27
  150.0 2.4 pad_maximum_fusion
  152.4 1.4 copy-done.10
  155.2 1.2 reshape.123
  156.4 3.5 %all-to-all-start.1 = ((bf16[8,2,16384]{2,1,0:T(2,128)(2,1)}), bf16[8,2,16384]{2,1,0:T(2,128)(2,1)S(1)}, u32[]{:S(2)}, u32[]{:S(2)}) async-start(bf16[8,2,16384]{2,1,0:T(2,128)(2,1)} %reshape.123), calls=%async_computation.1 | async-start | bytes 1048576 | tf_op jit(solution)/shard_map/all_to_all | solution.py:21
  159.9 19.2 %all-to-all-done.1 = bf16[8,2,16384]{2,1,0:T(2,128)(2,1)S(1)} async-done(((bf16[8,2,16384]{2,1,0:T(2,128)(2,1)}), bf16[8,2,16384]{2,1,0:T(2,128)(2,1)S(1)}, u32[]{:S(2)}, u32[]{:S(2)}) %all-to-all-start.1) | async-done | bytes 524320 | tf_op jit(solution)/shard_map/all_to_all | solution.py:21
  180.4 120.9 %all-reduce.2.cloned.1.call-done = f32[512,2048]{0,1:T(8,128)} async-done(((f32[512,2048]{0,1:T(8,128)}), f32[512,2048]{0,1:T(8,128)}) %all-reduce.2.cloned.1.call-update) | async-done | bytes 4194320 | tf_op jit(solution)/shard_map/psum | solution.py:118
  301.2 1.4 constant_dynamic-slice_fusion
  302.6 1.0 copy.11
  303.6 1.1 dynamic-slice.1
  (177 shorter events, 24.7 us)
Async XLA Ops:
  7.2 60.1 %copy-start = (bf16[1,256,512]{2,1,0:T(8,128)(2,1)S(1)}, bf16[1,256,512]{2,1,0:T(8,128)(2,1)}, u32[]{:S(2)}) copy-start(bf16[1,256,512]{2,1,0:T(8,128)(2,1)} %param.6) | copy-start | bytes 786436
  7.2 12.7 %copy-start.42 = (s32[1,8]{1,0:T(1,128)S(1)}, s32[1,8]{1,0:T(1,128)}, u32[]{:S(2)}) copy-start(s32[1,8]{1,0:T(1,128)} %param.11) | copy-start | bytes 100
  7.2 13.0 %copy-start.25 = (bf16[64,512]{1,0:T(8,128)(2,1)S(1)}, bf16[64,512]{1,0:T(8,128)(2,1)}, u32[]{:S(2)}) copy-start(bf16[64,512]{1,0:T(8,128)(2,1)} %param.9) | copy-start | bytes 196612
  7.2 60.1 %all-gather.2.cloned.1.call-start = ((), (), s32[]{:S(2)}) async-start(), calls=%async_computation.2 | async-start | bytes 1769472 | tf_op jit(solution)/shard_map/all_gather | solution.py:51
  11.2 58.1 %copy-start.43 = (s32[8]{0:T(128)}, s32[8]{0:T(128)S(1)}, u32[]{:S(2)}) copy-start(s32[8]{0:T(128)S(1)} %fusion.105) | copy-start | bytes 100
  12.6 53.0 %all-to-all-start = ((bf16[8,2,16384]{2,1,0:T(2,128)(2,1)}), bf16[8,2,16384]{2,1,0:T(2,128)(2,1)S(1)}, u32[]{:S(2)}, u32[]{:S(2)}) async-start(bf16[8,2,16384]{2,1,0:T(2,128)(2,1)} %reshape.119), calls=%async_computation | async-start | bytes 1048576 | tf_op jit(solution)/shard_map/all_to_all | solution.py:21
  19.9 281.4 %all-reduce.2.cloned.1.call-start = ((), (), s32[]{:S(2)}) async-start(), calls=%async_computation.3 | async-start | bytes 8388608 | tf_op jit(solution)/shard_map/psum | solution.py:118
  20.2 52.7 %copy-start.45 = (s32[8]{0:T(128)}, s32[8]{0:T(128)S(1)}, u32[]{:S(2)}) copy-start(s32[8]{0:T(128)S(1)} %multiply_add_fusion) | copy-start | bytes 100
  69.3 15.8 %copy-start.1 = (bf16[256,1536]{1,0:T(8,128)(2,1)}, bf16[256,1536]{1,0:T(8,128)(2,1)S(1)}, u32[]{:S(2)}) copy-start(bf16[256,1536]{1,0:T(8,128)(2,1)S(1)} %convolution_convert_fusion.4) | copy-start | bytes 2359300
  70.2 14.4 %collective-permute-start = (bf16[256,1024]{1,0:T(8,128)(2,1)}, bf16[256,1024]{1,0:T(8,128)(2,1)S(1)}, u32[]{:S(2)}, u32[]{:S(2)}) collective-permute-start(bf16[256,1024]{1,0:T(8,128)(2,1)} %slice.187), channel_id=1, source_target_pairs={{0,4},{4,0},{8,12},{12,8},{16,20},{20,16},{24,28},{28,24},{1,5},{5... | collective-permute-start | bytes 1572872 | tf_op jit(solution)/shard_map/ppermute | solution.py:17
  73.2 16.6 %copy-start.23 = (bf16[256,512]{1,0:T(8,128)(2,1)}, bf16[256,512]{1,0:T(8,128)(2,1)S(1)}, u32[]{:S(2)}) copy-start(bf16[256,512]{1,0:T(8,128)(2,1)S(1)} %convolution_convert_fusion.6) | copy-start | bytes 786436
  85.4 37.8 %copy-start.8 = (f32[256,512]{1,0:T(8,128)}, f32[256,512]{1,0:T(8,128)S(1)}, u32[]{:S(2)}) copy-start(f32[256,512]{1,0:T(8,128)S(1)} %get-tuple-element.42) | copy-start | bytes 1572868
  85.7 37.5 %copy-start.30 = (f32[256]{0:T(256)}, f32[256]{0:T(256)S(1)}, u32[]{:S(2)}) copy-start(f32[256]{0:T(256)S(1)} %fusion.25) | copy-start | bytes 3076
  91.3 30.0 %copy-start.7 = (f32[256,512]{1,0:T(8,128)}, f32[256,512]{1,0:T(8,128)S(1)}, u32[]{:S(2)}) copy-start(f32[256,512]{1,0:T(8,128)S(1)} %get-tuple-element.18) | copy-start | bytes 1572868
  91.3 30.0 %copy-start.29 = (f32[256]{0:T(256)}, f32[256]{0:T(256)S(1)}, u32[]{:S(2)}) copy-start(f32[256]{0:T(256)S(1)} %get-tuple-element.17) | copy-start | bytes 3076
  91.6 29.7 %copy-start.41 = (f32[256]{0:T(256)}, f32[256]{0:T(256)S(1)}, u32[]{:S(2)}) copy-start(f32[256]{0:T(256)S(1)} %fusion.13) | copy-start | bytes 3076
  96.2 25.4 %copy-start.5 = (f32[256,512]{1,0:T(8,128)}, f32[256,512]{1,0:T(8,128)S(1)}, u32[]{:S(2)}) copy-start(f32[256,512]{1,0:T(8,128)S(1)} %get-tuple-element.22) | copy-start | bytes 1572868
  96.3 25.4 %copy-start.28 = (f32[256]{0:T(256)}, f32[256]{0:T(256)S(1)}, u32[]{:S(2)}) copy-start(f32[256]{0:T(256)S(1)} %get-tuple-element.21) | copy-start | bytes 3076
  96.5 25.1 %copy-start.40 = (f32[256]{0:T(256)}, f32[256]{0:T(256)S(1)}, u32[]{:S(2)}) copy-start(f32[256]{0:T(256)S(1)} %fusion.15) | copy-start | bytes 3076
  101.0 20.9 %copy-start.3 = (f32[256,512]{1,0:T(8,128)}, f32[256,512]{1,0:T(8,128)S(1)}, u32[]{:S(2)}) copy-start(f32[256,512]{1,0:T(8,128)S(1)} %get-tuple-element.26) | copy-start | bytes 1572868
  101.1 20.9 %copy-start.26 = (f32[256]{0:T(256)}, f32[256]{0:T(256)S(1)}, u32[]{:S(2)}) copy-start(f32[256]{0:T(256)S(1)} %get-tuple-element.25) | copy-start | bytes 3076
  101.3 20.7 %copy-start.38 = (f32[256]{0:T(256)}, f32[256]{0:T(256)S(1)}, u32[]{:S(2)}) copy-start(f32[256]{0:T(256)S(1)} %fusion.17) | copy-start | bytes 3076
  106.1 16.1 %copy-start.36 = (f32[256]{0:T(256)}, f32[256]{0:T(256)S(1)}, u32[]{:S(2)}) copy-start(f32[256]{0:T(256)S(1)} %fusion.19) | copy-start | bytes 3076
  111.0 11.6 %copy-start.34 = (f32[256]{0:T(256)}, f32[256]{0:T(256)S(1)}, u32[]{:S(2)}) copy-start(f32[256]{0:T(256)S(1)} %fusion.21) | copy-start | bytes 3076
  115.9 7.0 %copy-start.32 = (f32[256]{0:T(256)}, f32[256]{0:T(256)S(1)}, u32[]{:S(2)}) copy-start(f32[256]{0:T(256)S(1)} %fusion.23) | copy-start | bytes 3076
  115.9 4.5 %copy-start.2 = (bf16[256,1536]{1,0:T(8,128)(2,1)S(1)}, bf16[256,1536]{1,0:T(8,128)(2,1)}, u32[]{:S(2)}) copy-start(bf16[256,1536]{1,0:T(8,128)(2,1)} %copy-done.1) | copy-start | bytes 2359300
  116.8 4.5 %copy-start.24 = (bf16[256,512]{1,0:T(8,128)(2,1)S(1)}, bf16[256,512]{1,0:T(8,128)(2,1)}, u32[]{:S(2)}) copy-start(bf16[256,512]{1,0:T(8,128)(2,1)} %copy-done.23) | copy-start | bytes 786436
  125.2 22.2 %collective-permute-start.2 = (bf16[256,512]{0,1:T(8,128)(2,1)}, bf16[256,512]{0,1:T(8,128)(2,1)}, u32[]{:S(2)}, u32[]{:S(2)}) collective-permute-start(bf16[256,512]{0,1:T(8,128)(2,1)} %slice.454), channel_id=1, source_target_pairs={{0,4},{4,0},{8,12},{12,8},{16,20},{20,16},{24,28},{28,24},{1,5},{5... | collective-permute-start | bytes 786440 | tf_op jit(solution)/shard_map/ppermute | solution.py:17
  128.9 4.1 %copy-start.6 = (f32[256,512]{1,0:T(8,128)S(1)}, f32[256,512]{1,0:T(8,128)}, u32[]{:S(2)}) copy-start(f32[256,512]{1,0:T(8,128)} %copy-done.5) | copy-start | bytes 1572868
  128.9 4.1 %copy-start.22 = (f32[256,512]{1,0:T(8,128)S(1)}, f32[256,512]{1,0:T(8,128)}, u32[]{:S(2)}) copy-start(f32[256,512]{1,0:T(8,128)} %get-tuple-element.24) | copy-start | bytes 1572868
  128.9 6.1 %copy-start.4 = (f32[256,512]{1,0:T(8,128)S(1)}, f32[256,512]{1,0:T(8,128)}, u32[]{:S(2)}) copy-start(f32[256,512]{1,0:T(8,128)} %copy-done.3) | copy-start | bytes 1572868
  128.9 6.1 %copy-start.21 = (f32[256,512]{1,0:T(8,128)S(1)}, f32[256,512]{1,0:T(8,128)}, u32[]{:S(2)}) copy-start(f32[256,512]{1,0:T(8,128)} %get-tuple-element.28) | copy-start | bytes 1572868
  128.9 6.1 %copy-start.27 = (f32[256]{0:T(256)S(1)}, f32[256]{0:T(256)}, u32[]{:S(2)}) copy-start(f32[256]{0:T(256)} %copy-done.26) | copy-start | bytes 3076
  129.0 6.1 %copy-start.39 = (f32[256]{0:T(256)S(1)}, f32[256]{0:T(256)}, u32[]{:S(2)}) copy-start(f32[256]{0:T(256)} %copy-done.38) | copy-start | bytes 3076
  129.0 6.1 %copy-start.51 = (f32[256]{0:T(256)S(1)}, f32[256]{0:T(256)}, u32[]{:S(2)}) copy-start(f32[256]{0:T(256)} %get-tuple-element.27) | copy-start | bytes 3076
  131.8 4.7 %copy-start.20 = (f32[256,512]{1,0:T(8,128)S(1)}, f32[256,512]{1,0:T(8,128)}, u32[]{:S(2)}) copy-start(f32[256,512]{1,0:T(8,128)} %get-tuple-element.32) | copy-start | bytes 1572868
  131.9 4.7 %copy-start.37 = (f32[256]{0:T(256)S(1)}, f32[256]{0:T(256)}, u32[]{:S(2)}) copy-start(f32[256]{0:T(256)} %copy-done.36) | copy-start | bytes 3076
  131.9 4.7 %copy-start.50 = (f32[256]{0:T(256)S(1)}, f32[256]{0:T(256)}, u32[]{:S(2)}) copy-start(f32[256]{0:T(256)} %get-tuple-element.31) | copy-start | bytes 3076
  134.0 3.9 %copy-start.19 = (f32[256,512]{1,0:T(8,128)S(1)}, f32[256,512]{1,0:T(8,128)}, u32[]{:S(2)}) copy-start(f32[256,512]{1,0:T(8,128)} %get-tuple-element.36) | copy-start | bytes 1572868
  134.0 3.9 %copy-start.35 = (f32[256]{0:T(256)S(1)}, f32[256]{0:T(256)}, u32[]{:S(2)}) copy-start(f32[256]{0:T(256)} %copy-done.34) | copy-start | bytes 3076
  135.3 4.0 %copy-start.9 = (f32[256,512]{1,0:T(8,128)S(1)}, f32[256,512]{1,0:T(8,128)}, u32[]{:S(2)}) copy-start(f32[256,512]{1,0:T(8,128)} %copy-done.8) | copy-start | bytes 1572868
  135.3 4.0 %copy-start.17 = (f32[256,512]{1,0:T(8,128)S(1)}, f32[256,512]{1,0:T(8,128)}, u32[]{:S(2)}) copy-start(f32[256,512]{1,0:T(8,128)} %get-tuple-element.44) | copy-start | bytes 1572868
  135.3 4.0 %copy-start.31 = (f32[256]{0:T(256)S(1)}, f32[256]{0:T(256)}, u32[]{:S(2)}) copy-start(f32[256]{0:T(256)} %copy-done.30) | copy-start | bytes 3076
  135.3 4.0 %copy-start.47 = (f32[256]{0:T(256)S(1)}, f32[256]{0:T(256)}, u32[]{:S(2)}) copy-start(f32[256]{0:T(256)} %get-tuple-element.43) | copy-start | bytes 3076
  139.3 8.1 %copy-start.16 = (f32[512,512]{0,1:T(8,128)S(1)}, f32[512,512]{0,1:T(8,128)}, u32[]{:S(2)}) copy-start(f32[512,512]{0,1:T(8,128)} %copy-done.15) | copy-start | bytes 3145732
  140.4 7.0 %collective-permute-start.1 = (bf16[256,512]{0,1:T(8,128)(2,1)S(1)}, bf16[256,512]{0,1:T(8,128)(2,1)S(1)}, u32[]{:S(2)}, u32[]{:S(2)}) collective-permute-start(bf16[256,512]{0,1:T(8,128)(2,1)S(1)} %slice.455), channel_id=1, source_target_pairs={{0,4},{4,0},{8,12},{12,8},{16,20},{20,16},{24,28},{28,24},{1,5},{5... | collective-permute-start | bytes 786440 | tf_op jit(solution)/shard_map/ppermute | solution.py:17
  154.0 25.3 %copy-start.44 = (s32[8]{0:T(128)S(1)}, s32[8]{0:T(128)}, u32[]{:S(2)}) copy-start(s32[8]{0:T(128)} %copy-done.43) | copy-start | bytes 100
  156.4 22.7 %all-to-all-start.1 = ((bf16[8,2,16384]{2,1,0:T(2,128)(2,1)}), bf16[8,2,16384]{2,1,0:T(2,128)(2,1)S(1)}, u32[]{:S(2)}, u32[]{:S(2)}) async-start(bf16[8,2,16384]{2,1,0:T(2,128)(2,1)} %reshape.123), calls=%async_computation.1 | async-start | bytes 1048576 | tf_op jit(solution)/shard_map/all_to_all | solution.py:21
  (11 other events, 25.7 us)
Sparse Core Ops, SparseCore 0:
  10.2 57.0 all-gather.1
  152.5 148.6 all-reduce.1
where the time goes:
time: 313 us; the launch traced here: 312 us
  waiting for transfers between devices  160 us (51%)
  matrix products  49.1 us (16%)
  blocking collectives  45.5 us (15%)
  local copies, waits for them, and re-layouts  16.5 us (5%)
  starting transfers between devices  15.1 us (5%)
  between operations  14.9 us (5%)
  other arithmetic  11.5 us (4%)
    psum x1, waiting for transfers between devices, per_device(): total = lax.psum(term, ('rows', 'rep'))  121 us
    all_gather x1, blocking collectives, per_device(): lax.all_gather(proj_weight, 'rows', axis=0, tiled=True)  45.5 us
    dot_general x18, matrix products, contract_cols(): lax.dot_general(left, right, (((1,), (1,)), ((), ())), preferred_element_...  25.6 us
    all_to_all x2, waiting for transfers between devices, move_blocks(): lax.all_to_all(outgoing, 'rows', split_axis=0, concat_axis=0, tiled=True)  19.2 us
    ppermute x3, waiting for transfers between devices, from_partner(): return lax.ppermute(block, axis, route)  17.6 us
    all_to_all x2, starting transfers between devices, move_blocks(): lax.all_to_all(outgoing, 'rows', split_axis=0, concat_axis=0, tiled=True)  10.7 us
    dot_general x20, matrix products, contract_rows(): lax.dot_general(left, right, (((0,), (0,)), ((), ())), preferred_element_...  7.68 us
    dot_general x8, matrix products, per_device(): jnp.dot(probs_b, v_head, preferred_element_type=jnp.float32)  7.63 us
  transfers between devices with their start and end apart: 7, of which 5 were waited for; matrix products, arithmetic and copies ran while one was open for 7% of the time, Pallas kernels for 0%

commit v1 on v0

--- a/solution.py
+++ b/solution.py
@@ -1,6 +1,8 @@
 import jax
 import jax.numpy as jnp
 from jax import lax
+from jax.experimental import pallas as pl
+from jax.experimental.pallas import tpu as pltpu
 from jax.sharding import PartitionSpec as P
 
 HEADS = 8
@@ -39,7 +41,7 @@
     )
 
 
-def per_device(feats, grad_out, qkv_weight, proj_weight, to_hilbert, to_zorder):
+def per_device_general(feats, grad_out, qkv_weight, proj_weight, to_hilbert, to_zorder):
     peer_count = lax.axis_size("rows")
     feature = feats[0]
     rows_dev, channels = feature.shape
@@ -120,6 +122,322 @@
     return (grad_z[None], owned[:, : 3 * channels], owned[:, 3 * channels :])
 
 
+MESH = pl.DeviceIdType.MESH
+PAIR = 128
+STRIP = 16
+F32 = jnp.float32
+BF16 = jnp.bfloat16
+
+
+def dot(left, right):
+    return jnp.dot(left, right, preferred_element_type=F32)
+
+
+def fused_kernel(peers, slot_rows, feats_ref, grad_ref, wq_ref, wp_ref, srow_ref, rrow_ref,
+                 gf_ref, qg_ref, pg_ref,
+                 wf, wz_s, wz_r, wx_s, wx_r, wy_s, wy_r, wc_s, wc_r,
+                 out_buf, arr_buf, sl_s, sl_r, back_buf, ret_buf, bk_s, bk_r,
+                 fa, ft, ff_s, ff_r, q_v, k_v, v_v, g_v, h_v, at_v, dq_v, dk_v, dv_v,
+                 dks, dkr, dk_s, dk_r, red_s, red_r, *reds):
+    rows, channels = feats_ref.shape
+    pairs = channels // PAIR
+    r = lax.axis_index("rows")
+    p = lax.axis_index("rep")
+    x, z = lax.rem(r, 2), lax.div(r, 2)
+    c, y = lax.rem(p, 2), lax.div(p, 2)
+    across_x = (r + 1 - 2 * x, p)
+    across_c = (r, p + 1 - 2 * c)
+    across_y = (r, p + 2 - 4 * y)
+    zs = peers // 2
+    sends = []
+
+    def send(src, dst, send_sem, recv_sem, device):
+        copy = pltpu.make_async_remote_copy(
+            src_ref=src, dst_ref=dst, send_sem=send_sem, recv_sem=recv_sem,
+            device_id=device, device_id_type=MESH)
+        copy.start()
+        sends.append(copy)
+        return copy
+
+    barrier = pltpu.get_barrier_semaphore()
+    for k in range(1, peers):
+        pl.semaphore_signal(barrier, inc=1, device_id=(lax.rem(r + k, peers), p), device_id_type=MESH)
+    for k in range(1, 4):
+        pl.semaphore_signal(barrier, inc=1, device_id=(r, lax.rem(p + k, 4)), device_id_type=MESH)
+
+    wide = wq_ref.shape[1]
+    for strip in range(4):
+        wf[r, strip, :, 0:wide] = wq_ref[strip * STRIP : (strip + 1) * STRIP, :]
+        wf[r, strip, :, wide:] = wp_ref[strip * STRIP : (strip + 1) * STRIP, :]
+    slot_ids = lax.broadcasted_iota(jnp.int32, (slot_rows, rows), 0)
+    pack = jnp.where(slot_ids == srow_ref[...], 1.0, 0.0).astype(BF16)
+    per_peer = slot_rows // peers
+    out_buf[...] = dot(pack, grad_ref[...]).astype(BF16).reshape(peers, per_peer, channels)
+    arr_buf[r] = out_buf[r]
+    fa[0] = feats_ref[...]
+    pl.semaphore_wait(barrier, peers - 1 + 3)
+
+    z_copies = []
+    for k in range(1, zs):
+        to = (lax.rem(z + k, zs) * 2 + x, p)
+        z_copies.append(send(wf.at[r, p], wf.at[r, p], wz_s.at[k - 1], wz_r.at[k - 1], to))
+    x_copies = [send(wf.at[r, p], wf.at[r, p], wx_s.at[0], wx_r.at[0], across_x)]
+    f_copy = send(feats_ref, fa.at[1], ff_s, ff_r, across_x)
+    slot_copies = []
+    for k in range(1, peers):
+        d = lax.rem(r + k, peers)
+        slot_copies.append(send(out_buf.at[d], arr_buf.at[r], sl_s.at[k - 1], sl_r.at[k - 1], (d, p)))
+    y_copies, c_copies = [], []
+
+    def to_y(row):
+        i = len(y_copies)
+        y_copies.append((send(wf.at[row, p], wf.at[row, p], wy_s.at[i], wy_r.at[i], across_y), row))
+
+    def to_c(row, strip):
+        i = len(c_copies)
+        c_copies.append(send(wf.at[row, strip], wf.at[row, strip], wc_s.at[i], wc_r.at[i], across_c))
+
+    for k in range(1, zs):
+        z_copies[k - 1].wait_recv()
+        row = lax.rem(z + zs - k, zs) * 2 + x
+        x_copies.append(send(wf.at[row, p], wf.at[row, p], wx_s.at[k], wx_r.at[k], across_x))
+        to_y(row)
+        to_c(row, p)
+    for k in range(zs):
+        x_copies[k].wait_recv()
+        row = lax.rem(z + zs - k, zs) * 2 + 1 - x
+        to_y(row)
+        to_c(row, p)
+    f_copy.wait_recv()
+    for i in range(2):
+        ft[:, i * rows : (i + 1) * rows] = fa[i].astype(F32).T.astype(BF16)
+    for copy, row in y_copies:
+        copy.wait_recv()
+        to_c(row, p + 2 - 4 * y)
+    for copy in slot_copies:
+        copy.wait_recv()
+    place = jnp.where(slot_ids == rrow_ref[...], 1.0, 0.0).astype(BF16)
+    h_v[...] = contract_rows(place, arr_buf[...].reshape(slot_rows, channels)).astype(BF16)
+    for copy in c_copies:
+        copy.wait_recv()
+
+    def weight(lo, hi):
+        return wf[:, :, :, lo:hi].reshape(4 * STRIP * peers, hi - lo)
+
+    q_v[...] = dot(feats_ref[...], weight(0, channels)).astype(BF16)
+    for i in range(2):
+        part = slice(i * rows, (i + 1) * rows)
+        k_v[part, :] = dot(fa[i], weight(channels, 2 * channels)).astype(BF16)
+        v_v[part, :] = dot(fa[i], weight(2 * channels, 3 * channels)).astype(BF16)
+    g_v[...] = contract_cols(h_v[...], weight(3 * channels, 4 * channels)).astype(BF16)
+
+    head_size = channels // HEADS
+    scale = head_size ** (-0.5)
+    log2e = 1.4426950408889634
+    lane = lax.broadcasted_iota(jnp.int32, (1, PAIR), 1)
+    masks = [jnp.where(lane < head_size, 1.0, 0.0).astype(BF16), jnp.where(lane < head_size, 0.0, 1.0).astype(BF16)]
+    chunks = [reds[9 * i : 9 * i + 9] for i in range(pairs + 1)]
+    flights = [{} for _ in chunks]
+
+    def spread(ch, lo, value):
+        term = chunks[ch][0]
+        value = value.astype(BF16)
+        hi = lo + value.shape[1]
+        for i in range(4 * peers):
+            cc, yy, xx, zz = i % 2, i // 2 % 2, i // 4 % 2, i // 8
+            term[cc, yy, xx, zz, :, lo:hi] = value[i * STRIP : (i + 1) * STRIP, :]
+
+    def sem(ch, i):
+        return red_s.at[ch, i], red_r.at[ch, i]
+
+    def stage1(ch):
+        term, r1 = chunks[ch][0], chunks[ch][1]
+        flights[ch][1] = send(term.at[1 - c], r1, *sem(ch, 0), across_c)
+
+    def stage2(ch):
+        term, r1, s1, r2 = chunks[ch][:4]
+        flights[ch][1].wait_recv()
+        s1[...] = (term[c].astype(F32) + r1[...].astype(F32)).astype(BF16)
+        flights[ch][2] = send(s1.at[1 - y], r2, *sem(ch, 1), across_y)
+
+    def stage3(ch):
+        s1, r2, s2, r3 = chunks[ch][2:6]
+        flights[ch][2].wait_recv()
+        s2[...] = (s1[y].astype(F32) + r2[...].astype(F32)).astype(BF16)
+        flights[ch][3] = send(s2.at[1 - x], r3, *sem(ch, 2), across_x)
+
+    def stage4(ch):
+        s2, r3, s3, r4 = chunks[ch][4:8]
+        flights[ch][3].wait_recv()
+        s3[...] = (s2[x].astype(F32) + r3[...].astype(F32)).astype(BF16)
+        flights[ch][4] = []
+        for k in range(1, zs):
+            zz = lax.rem(z + k, zs)
+            flights[ch][4].append(send(s3.at[zz], r4.at[k - 1], *sem(ch, 2 + k), (zz * 2 + x, p)))
+
+    def stage5(ch):
+        s3, r4, full = chunks[ch][6:9]
+        total = s3[z].astype(F32)
+        for k in range(1, zs):
+            flights[ch][4][k - 1].wait_recv()
+            total = total + r4[k - 1].astype(F32)
+        full[p] = total.astype(BF16)
+        flights[ch][5] = []
+        for k in range(1, 4):
+            flights[ch][5].append(send(full.at[p], full.at[p], *sem(ch, 2 + zs - 1 + k), (r, lax.rem(p + k, 4))))
+
+    def stage6(ch):
+        full = chunks[ch][8]
+        for copy in flights[ch][5]:
+            copy.wait_recv()
+        value = full[...].astype(F32).reshape(4 * STRIP, full.shape[2])
+        if ch < pairs:
+            for i in range(3):
+                lo = i * channels + ch * PAIR
+                qg_ref[:, lo : lo + PAIR] = value[:, i * PAIR : (i + 1) * PAIR]
+        else:
+            pg_ref[...] = value
+
+    stages = [stage1, stage2, stage3, stage4, stage5, stage6]
+
+    def tick(t):
+        for i, stage in enumerate(stages):
+            if 0 <= t - i <= pairs:
+                stage(t - i)
+
+    dk_copies = []
+    for hp in range(pairs):
+        cols = slice(hp * PAIR, (hp + 1) * PAIR)
+        qp, kp, vp, gp = q_v[:, cols], k_v[:, cols], v_v[:, cols], g_v[:, cols]
+        k_t = kp.astype(F32).T.astype(BF16)
+        v_t = vp.astype(F32).T.astype(BF16)
+        dk = dv = None
+        dq_t = []
+        for e in range(2):
+            mine = slice(e * head_size, (e + 1) * head_size)
+            qm, gm = qp * masks[e], gp * masks[e]
+            score = contract_cols(kp, qm)
+            raised = jnp.exp2((score - jnp.max(score, axis=0, keepdims=True)) * (scale * log2e))
+            probs = raised * (1.0 / jnp.sum(raised, axis=0, keepdims=True))
+            probs_b = probs.astype(BF16)
+            dprob = contract_cols(vp, gm)
+            delta = jnp.sum(probs * dprob, axis=0, keepdims=True)
+            dscore = (probs * (dprob - delta)).astype(BF16)
+            at_v[hp * PAIR + e * head_size : hp * PAIR + (e + 1) * head_size, :] = dot(v_t[mine], probs_b).astype(BF16)
+            dq_t.append(dot(k_t[mine], dscore))
+            dk_e, dv_e = dot(dscore, qm), dot(probs_b, gm)
+            dk = dk_e if dk is None else dk + dk_e
+            dv = dv_e if dv is None else dv + dv_e
+        dq_b = (jnp.concatenate(dq_t, axis=0) * scale).T.astype(BF16)
+        dk = dk * scale
+        dk_b, dv_b = dk.astype(BF16), dv.astype(BF16)
+        dks[hp, 0] = dk_b[rows:]
+        dks[hp, 1] = dv_b[rows:]
+        dk_copies.append(send(dks.at[hp], dkr.at[hp], dk_s.at[hp], dk_r.at[hp], across_x))
+        dq_v[:, cols] = dq_b
+        dk_v[:, cols] = dk[:rows]
+        dv_v[:, cols] = dv[:rows]
+        spread(hp, 0, dot(ft[:, 0:rows], dq_b))
+        spread(hp, PAIR, dot(ft[...], dk_b))
+        spread(hp, 2 * PAIR, dot(ft[...], dv_b))
+        tick(hp)
+    spread(pairs, 0, dot(at_v[...], h_v[...]))
+    tick(pairs)
+    hfeat = contract_cols(dq_v[...], weight(0, channels))
+    for hp in range(pairs):
+        cols = slice(hp * PAIR, (hp + 1) * PAIR)
+        dk_copies[hp].wait_recv()
+        dk_v[:, cols] = dk_v[:, cols] + dkr[hp, 0].astype(F32)
+        dv_v[:, cols] = dv_v[:, cols] + dkr[hp, 1].astype(F32)
+    hfeat = hfeat + contract_cols(dk_v[...].astype(BF16), weight(channels, 2 * channels))
+    hfeat = hfeat + contract_cols(dv_v[...].astype(BF16), weight(2 * channels, 3 * channels))
+    place = jnp.where(slot_ids == rrow_ref[...], 1.0, 0.0).astype(BF16)
+    back_buf[...] = dot(place, hfeat.astype(BF16)).astype(BF16).reshape(peers, per_peer, channels)
+    ret_buf[r] = back_buf[r]
+    back_copies = []
+    for k in range(1, peers):
+        d = lax.rem(r + k, peers)
+        back_copies.append(send(back_buf.at[d], ret_buf.at[r], bk_s.at[k - 1], bk_r.at[k - 1], (d, p)))
+    for t in range(pairs + 1, pairs + 4):
+        tick(t)
+    for copy in back_copies:
+        copy.wait_recv()
+    pack = jnp.where(slot_ids == srow_ref[...], 1.0, 0.0).astype(BF16)
+    gf_ref[...] = contract_rows(pack, ret_buf[...].reshape(slot_rows, channels)).astype(BF16)
+    for t in range(pairs + 4, pairs + len(stages)):
+        tick(t)
+    for copy in sends:
+        copy.wait_send()
+
+
+def per_device(feats, grad_out, qkv_weight, proj_weight, to_hilbert, to_zorder):
+    peers = lax.axis_size("rows")
+    feature = feats[0]
+    rows, channels = feature.shape
+    blocks = to_hilbert.shape[1]
+    block = rows // blocks
+    forward_list, inverse_list = to_hilbert[0], to_zorder[0]
+    target = forward_list // blocks
+    send_slot = target * CAP + rank_within(jnp.arange(blocks, dtype=jnp.int32), target)
+    source = inverse_list // blocks
+    recv_slot = source * CAP + rank_within(inverse_list, source)
+    within = jnp.arange(block, dtype=jnp.int32)
+    srow = (send_slot[:, None] * block + within[None, :]).reshape(1, rows)
+    rrow = (recv_slot[:, None] * block + within[None, :]).reshape(1, rows)
+    slot_rows = peers * CAP * block
+    zs = peers // 2
+    pairs = channels // PAIR
+    wide = qkv_weight.shape[1] + channels
+    dma = pltpu.SemaphoreType.DMA
+
+    def vm(*shape, kind=BF16):
+        return pltpu.VMEM(shape, kind)
+
+    scratch = [
+        vm(peers, 4, STRIP, wide),
+        dma((zs - 1,)), dma((zs - 1,)), dma((zs,)), dma((zs,)),
+        dma((peers - 1,)), dma((peers - 1,)), dma((2 * peers - 2,)), dma((2 * peers - 2,)),
+        vm(peers, slot_rows // peers, channels), vm(peers, slot_rows // peers, channels),
+        dma((peers - 1,)), dma((peers - 1,)),
+        vm(peers, slot_rows // peers, channels), vm(peers, slot_rows // peers, channels),
+        dma((peers - 1,)), dma((peers - 1,)),
+        vm(2, rows, channels), vm(channels, 2 * rows), dma, dma,
+        vm(rows, channels), vm(2 * rows, channels), vm(2 * rows, channels), vm(rows, channels), vm(rows, channels),
+        vm(channels, rows), vm(rows, channels), vm(rows, channels, kind=F32), vm(rows, channels, kind=F32),
+        vm(pairs, 2, rows, PAIR), vm(pairs, 2, rows, PAIR), dma((pairs,)), dma((pairs,)),
+        dma((pairs + 1, zs + 5)), dma((pairs + 1, zs + 5)),
+    ]
+    for ch in range(pairs + 1):
+        w = 3 * PAIR if ch < pairs else channels
+        scratch += [vm(2, 2, 2, zs, STRIP, w), vm(2, 2, zs, STRIP, w), vm(2, 2, zs, STRIP, w),
+                    vm(2, zs, STRIP, w), vm(2, zs, STRIP, w), vm(zs, STRIP, w), vm(zs, STRIP, w),
+                    vm(zs - 1, STRIP, w), vm(4, STRIP, w)]
+
+    def body(*refs):
+        fused_kernel(peers, slot_rows, *refs)
+
+    share = qkv_weight.shape[0]
+    grad_z, qkv_grad, proj_grad = pl.pallas_call(
+        body,
+        out_shape=(
+            jax.ShapeDtypeStruct((rows, channels), BF16),
+            jax.ShapeDtypeStruct((share, qkv_weight.shape[1]), F32),
+            jax.ShapeDtypeStruct((share, channels), F32),
+        ),
+        in_specs=[pl.BlockSpec(memory_space=pltpu.VMEM)] * 6,
+        out_specs=(pl.BlockSpec(memory_space=pltpu.VMEM),) * 3,
+        scratch_shapes=scratch,
+        compiler_params=pltpu.CompilerParams(
+            collective_id=0, has_side_effects=True, vmem_limit_bytes=48 * 1024 * 1024
+        ),
+    )(feature, grad_out[0], qkv_weight, proj_weight, srow, rrow)
+    return grad_z[None], qkv_grad, proj_grad
+
+
+def fits_kernel(mesh):
+    return mesh.shape["rows"] == 8 and mesh.shape["rep"] == 4
+
+
 def solution(mesh):
     placed = (
         P("rep", "rows", None),
@@ -130,7 +448,7 @@
         P("rep", "rows"),
     )
     return jax.shard_map(
-        per_device,
+        per_device if fits_kernel(mesh) else per_device_general,
         mesh=mesh,
         in_specs=placed,
         out_specs=(P("rep", "rows", None), P("rows", None), P("rows", None)),

time: 313 us -> 79.2 us (0.25)
  waiting for transfers between devices: 160 us -> 0 us
  Pallas kernels: 0 us -> 70.5 us
  matrix products: 49.1 us -> 0 us
  blocking collectives: 45.5 us -> 0 us
  starting transfers between devices: 15.1 us -> 0 us
  between operations: 14.9 us -> 0.67 us
  other arithmetic: 11.5 us -> 0.58 us
  local copies, waits for them, and re-layouts: 16.5 us -> 7.22 us
    psum x1 -> x0, waiting for transfers between devices: 121 us -> none  [per_device(): total = lax.psum(term, ('rows', 'rep'))]
    pallas_call x0 -> x1, Pallas kernels: none -> 70.5 us  [per_device(): pl.pallas_call(body, out_shape=(jax.ShapeDtypeStruct((rows, channels), BF...]
    dot_general x57 -> x0, matrix products: 49.1 us -> none  [the longest x18 25.6 us: contract_cols(): lax.dot_general(left, right, (((1,), (1,)), ((), ())), preferred_element_...]
    all_gather x1 -> x0, blocking collectives: 45.5 us -> none  [per_device(): lax.all_gather(proj_weight, 'rows', axis=0, tiled=True)]
    all_to_all x2 -> x0, waiting for transfers between devices: 19.2 us -> none  [move_blocks(): lax.all_to_all(outgoing, 'rows', split_axis=0, concat_axis=0, tiled=True)]
    ppermute x3 -> x0, waiting for transfers between devices: 17.6 us -> none  [from_partner(): return lax.ppermute(block, axis, route)]
    all_to_all x2 -> x0, starting transfers between devices: 10.7 us -> none  [move_blocks(): lax.all_to_all(outgoing, 'rows', split_axis=0, concat_axis=0, tiled=True)]
    ppermute x3 -> x0, starting transfers between devices: 4.3 us -> none  [from_partner(): return lax.ppermute(block, axis, route)]
  transfers between devices with their start and end apart: 7 -> 0, of which waited for: 5 -> 0; matrix products, arithmetic and copies ran while one was open for 7% -> 0% of each run, Pallas kernels for 0% -> 0%
where the time goes in v1:
time: 79.2 us; the launch traced here: 78.9 us
  Pallas kernels  70.5 us (89%)
  local copies, waits for them, and re-layouts  7.22 us (9%)
    pallas_call x1, Pallas kernels, per_device(): pl.pallas_call(body, out_shape=(jax.ShapeDtypeStruct((rows, channels), BF...  70.5 us
    unnamed x15, local copies, waits for them, and re-layouts  7.06 us

profile of v1, /device:TPU:0, one launch (start us, length us, event | category | flops | bytes accessed | tf_op | source)
XLA Modules:
  0.0 78.9 jit_solution(10083709542476364685)
XLA Ops:
  0.6 0.0 copy-start.5
  0.6 0.6 copy-done.5
  1.3 0.2 convert_reduce_fusion.1
  1.5 0.0 copy-start.4
  1.5 0.6 copy-done.4
  2.2 0.2 convert_reduce_fusion
  2.4 0.1 iota_add_fusion
  2.4 0.1 add.87.refs_5_
  2.5 0.1 iota_add_fusion.1
  2.6 0.1 add.82.refs_4_
  2.7 0.0 copy-start
  2.7 1.0 %copy-done = bf16[1,256,512]{2,1,0:T(8,128)(2,1)S(1)} copy-done((bf16[1,256,512]{2,1,0:T(8,128)(2,1)S(1)}, bf16[1,256,512]{2,1,0:T(8,128)(2,1)}, u32[]{:S(2)}) %copy-start) | copy-done | bytes 262168
  3.6 0.0 copy-start.1
  3.6 0.9 %copy-done.1 = bf16[1,256,512]{2,1,0:T(8,128)(2,1)S(1)} copy-done((bf16[1,256,512]{2,1,0:T(8,128)(2,1)S(1)}, bf16[1,256,512]{2,1,0:T(8,128)(2,1)}, u32[]{:S(2)}) %copy-start.1) | copy-done | bytes 262168
  4.6 0.0 copy-start.2
  4.6 0.9 %copy-done.2 = bf16[64,1536]{1,0:T(8,128)(2,1)S(1)} copy-done((bf16[64,1536]{1,0:T(8,128)(2,1)S(1)}, bf16[64,1536]{1,0:T(8,128)(2,1)}, u32[]{:S(2)}) %copy-start.2) | copy-done | bytes 196632
  5.5 0.0 copy-start.3
  5.5 0.8 %copy-done.3 = bf16[64,512]{1,0:T(8,128)(2,1)S(1)} copy-done((bf16[64,512]{1,0:T(8,128)(2,1)S(1)}, bf16[64,512]{1,0:T(8,128)(2,1)}, u32[]{:S(2)}) %copy-start.3) | copy-done | bytes 65560
  6.3 70.5 %shard_map.85 = (bf16[256,512]{1,0:T(8,128)(2,1)S(1)}, f32[64,1536]{1,0:T(8,128)S(1)}, f32[64,512]{1,0:T(8,128)S(1)}) custom-call(bf16[256,512]{1,0:T(8,128)(2,1)S(1)} %bitcast.21, bf16[256,512]{1,0:T(8,128)(2,1)S(1)} %bitcast.22, bf16[64,1536]{1,0:T(8,128)(2,1)S(1)} %copy-done.2, bf16[64,512]{1,0:T(8,128)(2,1)S(1)} %copy-done.3, s32[1,256]{1,0:T(1,128)S(1)} %add.82.refs_4_, ...), custom_call_target="tpu_custom_call" | custom-call | tf_op jit(solution)/shard_map/pallas_call | solution.py:420
  76.8 0.7 copy.12
  77.5 0.7 copy.13
  78.3 0.7 copy.14
  (6 shorter events, 0.1 us)
Async XLA Ops:
  0.6 0.7 copy-start.5
  1.5 0.7 copy-start.4
  2.7 1.0 %copy-start = (bf16[1,256,512]{2,1,0:T(8,128)(2,1)S(1)}, bf16[1,256,512]{2,1,0:T(8,128)(2,1)}, u32[]{:S(2)}) copy-start(bf16[1,256,512]{2,1,0:T(8,128)(2,1)} %param.6) | copy-start | bytes 786436
  3.6 0.9 %copy-start.1 = (bf16[1,256,512]{2,1,0:T(8,128)(2,1)S(1)}, bf16[1,256,512]{2,1,0:T(8,128)(2,1)}, u32[]{:S(2)}) copy-start(bf16[1,256,512]{2,1,0:T(8,128)(2,1)} %param.7) | copy-start | bytes 786436
  4.6 0.9 %copy-start.2 = (bf16[64,1536]{1,0:T(8,128)(2,1)S(1)}, bf16[64,1536]{1,0:T(8,128)(2,1)}, u32[]{:S(2)}) copy-start(bf16[64,1536]{1,0:T(8,128)(2,1)} %refs_2_.1) | copy-start | bytes 589828
  5.5 0.8 %copy-start.3 = (bf16[64,512]{1,0:T(8,128)(2,1)S(1)}, bf16[64,512]{1,0:T(8,128)(2,1)}, u32[]{:S(2)}) copy-start(bf16[64,512]{1,0:T(8,128)(2,1)} %refs_3_.1) | copy-start | bytes 196612

commit v2 on v1

--- a/solution.py
+++ b/solution.py
@@ -133,13 +133,26 @@
     return jnp.dot(left, right, preferred_element_type=F32)
 
 
-def fused_kernel(peers, slot_rows, feats_ref, grad_ref, wq_ref, wp_ref, srow_ref, rrow_ref,
+def slot_of_row(owners, order_keys, block, rows):
+    lane = lax.broadcasted_iota(jnp.int32, (1, rows), 1)
+    out = lax.rem(lane, block)
+    for i, owner in enumerate(owners):
+        rank = jnp.int32(0)
+        for j, other in enumerate(owners):
+            if j != i:
+                rank += jnp.where(jnp.logical_and(other == owner, order_keys[j] < order_keys[i]), 1, 0)
+        out += jnp.where(lax.div(lane, block) == i, (owner * CAP + rank) * block, 0)
+    return out
+
+
+def fused_kernel(peers, slot_rows, feats_hbm, grad_hbm, wq_hbm, wp_hbm, toh_hbm, toz_hbm,
                  gf_ref, qg_ref, pg_ref,
                  wf, wz_s, wz_r, wx_s, wx_r, wy_s, wy_r, wc_s, wc_r,
                  out_buf, arr_buf, sl_s, sl_r, back_buf, ret_buf, bk_s, bk_r,
                  fa, ft, ff_s, ff_r, q_v, k_v, v_v, g_v, h_v, at_v, dq_v, dk_v, dv_v,
-                 dks, dkr, dk_s, dk_r, red_s, red_r, *reds):
-    rows, channels = feats_ref.shape
+                 dks, dkr, dk_s, dk_r, red_s, red_r, grad_v, toh, toz, in_sem, probs_v, *reds):
+    rows, channels = feats_hbm.shape
+    blocks = toh_hbm.shape[1]
     pairs = channels // PAIR
     r = lax.axis_index("rows")
     p = lax.axis_index("rep")
@@ -159,22 +172,35 @@
         sends.append(copy)
         return copy
 
+    wide = wq_hbm.shape[2]
+    loads = []
+    for i, (src, dst) in enumerate([(toh_hbm, toh), (toz_hbm, toz), (grad_hbm, grad_v),
+                                    (wq_hbm, wf.at[r, :, :, pl.ds(0, wide)]),
+                                    (wp_hbm, wf.at[r, :, :, pl.ds(wide, channels)]),
+                                    (feats_hbm, fa.at[0])]):
+        copy = pltpu.make_async_copy(src, dst, in_sem.at[i])
+        copy.start()
+        loads.append(copy)
     barrier = pltpu.get_barrier_semaphore()
     for k in range(1, peers):
         pl.semaphore_signal(barrier, inc=1, device_id=(lax.rem(r + k, peers), p), device_id_type=MESH)
     for k in range(1, 4):
         pl.semaphore_signal(barrier, inc=1, device_id=(r, lax.rem(p + k, 4)), device_id_type=MESH)
 
-    wide = wq_ref.shape[1]
-    for strip in range(4):
-        wf[r, strip, :, 0:wide] = wq_ref[strip * STRIP : (strip + 1) * STRIP, :]
-        wf[r, strip, :, wide:] = wp_ref[strip * STRIP : (strip + 1) * STRIP, :]
+    for copy in loads[:2]:
+        copy.wait()
+    forward_list = [toh[0, i] for i in range(blocks)]
+    inverse_list = [toz[0, i] for i in range(blocks)]
+    srow = slot_of_row([lax.div(b, blocks) for b in forward_list], list(range(blocks)), rows // blocks, rows)
+    rrow = slot_of_row([lax.div(b, blocks) for b in inverse_list], inverse_list, rows // blocks, rows)
     slot_ids = lax.broadcasted_iota(jnp.int32, (slot_rows, rows), 0)
-    pack = jnp.where(slot_ids == srow_ref[...], 1.0, 0.0).astype(BF16)
+    pack = jnp.where(slot_ids == srow, 1.0, 0.0).astype(BF16)
     per_peer = slot_rows // peers
-    out_buf[...] = dot(pack, grad_ref[...]).astype(BF16).reshape(peers, per_peer, channels)
+    loads[2].wait()
+    out_buf[...] = dot(pack, grad_v[...]).astype(BF16).reshape(peers, per_peer, channels)
     arr_buf[r] = out_buf[r]
-    fa[0] = feats_ref[...]
+    for copy in loads[3:]:
+        copy.wait()
     pl.semaphore_wait(barrier, peers - 1 + 3)
 
     z_copies = []
@@ -182,11 +208,7 @@
         to = (lax.rem(z + k, zs) * 2 + x, p)
         z_copies.append(send(wf.at[r, p], wf.at[r, p], wz_s.at[k - 1], wz_r.at[k - 1], to))
     x_copies = [send(wf.at[r, p], wf.at[r, p], wx_s.at[0], wx_r.at[0], across_x)]
-    f_copy = send(feats_ref, fa.at[1], ff_s, ff_r, across_x)
-    slot_copies = []
-    for k in range(1, peers):
-        d = lax.rem(r + k, peers)
-        slot_copies.append(send(out_buf.at[d], arr_buf.at[r], sl_s.at[k - 1], sl_r.at[k - 1], (d, p)))
+    f_copy = send(fa.at[0], fa.at[1], ff_s, ff_r, across_x)
     y_copies, c_copies = [], []
 
     def to_y(row):
@@ -203,6 +225,10 @@
         x_copies.append(send(wf.at[row, p], wf.at[row, p], wx_s.at[k], wx_r.at[k], across_x))
         to_y(row)
         to_c(row, p)
+    slot_copies = []
+    for k in range(1, peers):
+        d = lax.rem(r + k, peers)
+        slot_copies.append(send(out_buf.at[d], arr_buf.at[r], sl_s.at[k - 1], sl_r.at[k - 1], (d, p)))
     for k in range(zs):
         x_copies[k].wait_recv()
         row = lax.rem(z + zs - k, zs) * 2 + 1 - x
@@ -214,22 +240,17 @@
     for copy, row in y_copies:
         copy.wait_recv()
         to_c(row, p + 2 - 4 * y)
-    for copy in slot_copies:
-        copy.wait_recv()
-    place = jnp.where(slot_ids == rrow_ref[...], 1.0, 0.0).astype(BF16)
-    h_v[...] = contract_rows(place, arr_buf[...].reshape(slot_rows, channels)).astype(BF16)
     for copy in c_copies:
         copy.wait_recv()
 
     def weight(lo, hi):
         return wf[:, :, :, lo:hi].reshape(4 * STRIP * peers, hi - lo)
 
-    q_v[...] = dot(feats_ref[...], weight(0, channels)).astype(BF16)
+    q_v[...] = dot(fa[0], weight(0, channels)).astype(BF16)
     for i in range(2):
         part = slice(i * rows, (i + 1) * rows)
         k_v[part, :] = dot(fa[i], weight(channels, 2 * channels)).astype(BF16)
         v_v[part, :] = dot(fa[i], weight(2 * channels, 3 * channels)).astype(BF16)
-    g_v[...] = contract_cols(h_v[...], weight(3 * channels, 4 * channels)).astype(BF16)
 
     head_size = channels // HEADS
     scale = head_size ** (-0.5)
@@ -291,9 +312,9 @@
         for copy in flights[ch][5]:
             copy.wait_recv()
         value = full[...].astype(F32).reshape(4 * STRIP, full.shape[2])
-        if ch < pairs:
+        if ch > 0:
             for i in range(3):
-                lo = i * channels + ch * PAIR
+                lo = i * channels + (ch - 1) * PAIR
                 qg_ref[:, lo : lo + PAIR] = value[:, i * PAIR : (i + 1) * PAIR]
         else:
             pg_ref[...] = value
@@ -304,26 +325,43 @@
         for i, stage in enumerate(stages):
             if 0 <= t - i <= pairs:
                 stage(t - i)
+
+    for hp in range(pairs):
+        cols = slice(hp * PAIR, (hp + 1) * PAIR)
+        qp, kp = q_v[:, cols], k_v[:, cols]
+        v_t = v_v[:, cols].astype(F32).T.astype(BF16)
+        for e in range(2):
+            mine = slice(e * head_size, (e + 1) * head_size)
+            score = contract_cols(kp, qp * masks[e])
+            raised = jnp.exp2((score - jnp.max(score, axis=0, keepdims=True)) * (scale * log2e))
+            probs = raised * (1.0 / jnp.sum(raised, axis=0, keepdims=True))
+            probs_v[2 * hp + e] = probs
+            at_v[hp * PAIR + e * head_size : hp * PAIR + (e + 1) * head_size, :] = dot(
+                v_t[mine], probs.astype(BF16)).astype(BF16)
+
+    for copy in slot_copies:
+        copy.wait_recv()
+    place = jnp.where(slot_ids == rrow, 1.0, 0.0).astype(BF16)
+    h_v[...] = contract_rows(place, arr_buf[...].reshape(slot_rows, channels)).astype(BF16)
+    spread(0, 0, dot(at_v[...], h_v[...]))
+    tick(0)
+    g_v[...] = contract_cols(h_v[...], weight(3 * channels, 4 * channels)).astype(BF16)
 
     dk_copies = []
     for hp in range(pairs):
         cols = slice(hp * PAIR, (hp + 1) * PAIR)
         qp, kp, vp, gp = q_v[:, cols], k_v[:, cols], v_v[:, cols], g_v[:, cols]
         k_t = kp.astype(F32).T.astype(BF16)
-        v_t = vp.astype(F32).T.astype(BF16)
         dk = dv = None
         dq_t = []
         for e in range(2):
             mine = slice(e * head_size, (e + 1) * head_size)
             qm, gm = qp * masks[e], gp * masks[e]
-            score = contract_cols(kp, qm)
-            raised = jnp.exp2((score - jnp.max(score, axis=0, keepdims=True)) * (scale * log2e))
-            probs = raised * (1.0 / jnp.sum(raised, axis=0, keepdims=True))
+            probs = probs_v[2 * hp + e]
             probs_b = probs.astype(BF16)
             dprob = contract_cols(vp, gm)
             delta = jnp.sum(probs * dprob, axis=0, keepdims=True)
             dscore = (probs * (dprob - delta)).astype(BF16)
-            at_v[hp * PAIR + e * head_size : hp * PAIR + (e + 1) * head_size, :] = dot(v_t[mine], probs_b).astype(BF16)
             dq_t.append(dot(k_t[mine], dscore))
             dk_e, dv_e = dot(dscore, qm), dot(probs_b, gm)
             dk = dk_e if dk is None else dk + dk_e
@@ -337,21 +375,21 @@
         dq_v[:, cols] = dq_b
         dk_v[:, cols] = dk[:rows]
         dv_v[:, cols] = dv[:rows]
-        spread(hp, 0, dot(ft[:, 0:rows], dq_b))
-        spread(hp, PAIR, dot(ft[...], dk_b))
-        spread(hp, 2 * PAIR, dot(ft[...], dv_b))
-        tick(hp)
-    spread(pairs, 0, dot(at_v[...], h_v[...]))
-    tick(pairs)
+        spread(1 + hp, 0, dot(ft[:, 0:rows], dq_b))
+        spread(1 + hp, PAIR, dot(ft[...], dk_b))
+        spread(1 + hp, 2 * PAIR, dot(ft[...], dv_b))
+        tick(1 + hp)
     hfeat = contract_cols(dq_v[...], weight(0, channels))
-    for hp in range(pairs):
-        cols = slice(hp * PAIR, (hp + 1) * PAIR)
-        dk_copies[hp].wait_recv()
-        dk_v[:, cols] = dk_v[:, cols] + dkr[hp, 0].astype(F32)
-        dv_v[:, cols] = dv_v[:, cols] + dkr[hp, 1].astype(F32)
-    hfeat = hfeat + contract_cols(dk_v[...].astype(BF16), weight(channels, 2 * channels))
-    hfeat = hfeat + contract_cols(dv_v[...].astype(BF16), weight(2 * channels, 3 * channels))
-    place = jnp.where(slot_ids == rrow_ref[...], 1.0, 0.0).astype(BF16)
+    for lo, hi in ((0, pairs - 1), (pairs - 1, pairs)):
+        part = slice(lo * PAIR, hi * PAIR)
+        for hp in range(lo, hi):
+            cols = slice(hp * PAIR, (hp + 1) * PAIR)
+            dk_copies[hp].wait_recv()
+            dk_v[:, cols] = dk_v[:, cols] + dkr[hp, 0].astype(F32)
+            dv_v[:, cols] = dv_v[:, cols] + dkr[hp, 1].astype(F32)
+        hfeat += contract_cols(dk_v[:, part].astype(BF16), weight(channels + lo * PAIR, channels + hi * PAIR))
+        hfeat += contract_cols(dv_v[:, part].astype(BF16), weight(2 * channels + lo * PAIR, 2 * channels + hi * PAIR))
+    place = jnp.where(slot_ids == rrow, 1.0, 0.0).astype(BF16)
     back_buf[...] = dot(place, hfeat.astype(BF16)).astype(BF16).reshape(peers, per_peer, channels)
     ret_buf[r] = back_buf[r]
     back_copies = []
@@ -362,7 +400,7 @@
         tick(t)
     for copy in back_copies:
         copy.wait_recv()
-    pack = jnp.where(slot_ids == srow_ref[...], 1.0, 0.0).astype(BF16)
+    pack = jnp.where(slot_ids == srow, 1.0, 0.0).astype(BF16)
     gf_ref[...] = contract_rows(pack, ret_buf[...].reshape(slot_rows, channels)).astype(BF16)
     for t in range(pairs + 4, pairs + len(stages)):
         tick(t)
@@ -376,14 +414,6 @@
     rows, channels = feature.shape
     blocks = to_hilbert.shape[1]
     block = rows // blocks
-    forward_list, inverse_list = to_hilbert[0], to_zorder[0]
-    target = forward_list // blocks
-    send_slot = target * CAP + rank_within(jnp.arange(blocks, dtype=jnp.int32), target)
-    source = inverse_list // blocks
-    recv_slot = source * CAP + rank_within(inverse_list, source)
-    within = jnp.arange(block, dtype=jnp.int32)
-    srow = (send_slot[:, None] * block + within[None, :]).reshape(1, rows)
-    rrow = (recv_slot[:, None] * block + within[None, :]).reshape(1, rows)
     slot_rows = peers * CAP * block
     zs = peers // 2
     pairs = channels // PAIR
@@ -406,9 +436,11 @@
         vm(channels, rows), vm(rows, channels), vm(rows, channels, kind=F32), vm(rows, channels, kind=F32),
         vm(pairs, 2, rows, PAIR), vm(pairs, 2, rows, PAIR), dma((pairs,)), dma((pairs,)),
         dma((pairs + 1, zs + 5)), dma((pairs + 1, zs + 5)),
+        vm(rows, channels), pltpu.SMEM((1, blocks), jnp.int32), pltpu.SMEM((1, blocks), jnp.int32), dma((6,)),
+        vm(HEADS, 2 * rows, rows, kind=F32),
     ]
     for ch in range(pairs + 1):
-        w = 3 * PAIR if ch < pairs else channels
+        w = 3 * PAIR if ch > 0 else channels
         scratch += [vm(2, 2, 2, zs, STRIP, w), vm(2, 2, zs, STRIP, w), vm(2, 2, zs, STRIP, w),
                     vm(2, zs, STRIP, w), vm(2, zs, STRIP, w), vm(zs, STRIP, w), vm(zs, STRIP, w),
                     vm(zs - 1, STRIP, w), vm(4, STRIP, w)]
@@ -424,13 +456,13 @@
             jax.ShapeDtypeStruct((share, qkv_weight.shape[1]), F32),
             jax.ShapeDtypeStruct((share, channels), F32),
         ),
-        in_specs=[pl.BlockSpec(memory_space=pltpu.VMEM)] * 6,
+        in_specs=[pl.BlockSpec(memory_space=pltpu.HBM)] * 6,
         out_specs=(pl.BlockSpec(memory_space=pltpu.VMEM),) * 3,
         scratch_shapes=scratch,
         compiler_params=pltpu.CompilerParams(
             collective_id=0, has_side_effects=True, vmem_limit_bytes=48 * 1024 * 1024
         ),
-    )(feature, grad_out[0], qkv_weight, proj_weight, srow, rrow)
+    )(feature, grad_out[0], qkv_weight.reshape(4, STRIP, -1), proj_weight.reshape(4, STRIP, -1), to_hilbert, to_zorder)
     return grad_z[None], qkv_grad, proj_grad
 
 

time: 79.2 us -> 81.5 us (1.029)
  Pallas kernels: 70.5 us -> 74.2 us
    pallas_call x1, Pallas kernels: 70.5 us -> 74.2 us  [per_device(): pl.pallas_call(body, out_shape=(jax.ShapeDtypeStruct((rows, channels), BF...]
where the time goes in v2:
time: 81.5 us; the launch traced here: 81.3 us
  Pallas kernels  74.2 us (91%)
  local copies, waits for them, and re-layouts  6.43 us (8%)
    pallas_call x1, Pallas kernels, per_device(): pl.pallas_call(body, out_shape=(jax.ShapeDtypeStruct((rows, channels), BF...  74.2 us
    unnamed x15, local copies, waits for them, and re-layouts  6.43 us

profile of v2, /device:TPU:0, one launch (start us, length us, event | category | flops | bytes accessed | tf_op | source)
XLA Modules:
  0.0 81.3 jit_solution(18053184025858776444)
XLA Ops:
  0.6 0.0 copy-start.4
  0.6 0.0 copy-start.5
  0.7 0.6 copy-done.4
  1.3 0.0 copy-done.5
  1.3 0.0 copy-start
  1.3 0.9 %copy-done = bf16[1,256,512]{2,1,0:T(8,128)(2,1)S(1)} copy-done((bf16[1,256,512]{2,1,0:T(8,128)(2,1)S(1)}, bf16[1,256,512]{2,1,0:T(8,128)(2,1)}, u32[]{:S(2)}) %copy-start) | copy-done | bytes 262168
  2.3 0.0 copy-start.1
  2.3 0.9 %copy-done.1 = bf16[1,256,512]{2,1,0:T(8,128)(2,1)S(1)} copy-done((bf16[1,256,512]{2,1,0:T(8,128)(2,1)S(1)}, bf16[1,256,512]{2,1,0:T(8,128)(2,1)}, u32[]{:S(2)}) %copy-start.1) | copy-done | bytes 262168
  3.2 0.0 copy-start.2
  3.2 0.9 %copy-done.2 = bf16[64,1536]{1,0:T(8,128)(2,1)S(1)} copy-done((bf16[64,1536]{1,0:T(8,128)(2,1)S(1)}, bf16[64,1536]{1,0:T(8,128)(2,1)}, u32[]{:S(2)}) %copy-start.2) | copy-done | bytes 196632
  4.1 0.0 copy-start.3
  4.1 0.8 %copy-done.3 = bf16[64,512]{1,0:T(8,128)(2,1)S(1)} copy-done((bf16[64,512]{1,0:T(8,128)(2,1)S(1)}, bf16[64,512]{1,0:T(8,128)(2,1)}, u32[]{:S(2)}) %copy-start.3) | copy-done | bytes 65560
  5.0 74.2 %shard_map.85 = (bf16[256,512]{1,0:T(8,128)(2,1)S(1)}, f32[64,1536]{1,0:T(8,128)S(1)}, f32[64,512]{1,0:T(8,128)S(1)}) custom-call(bf16[256,512]{1,0:T(8,128)(2,1)S(1)} %bitcast.5, bf16[256,512]{1,0:T(8,128)(2,1)S(1)} %bitcast.6, bf16[4,16,1536]{2,1,0:T(8,128)(2,1)S(1)} %bitcast.8, bf16[4,16,512]{2,1,0:T(8,128)(2,1)S(1)} %bitcast.9, s32[1,8]{1,0:T(1,128)S(1)} %copy-done.4, ...), custom_call_target="tpu_custom_call" | custom-call | tf_op jit(solution)/shard_map/pallas_call | solution.py:452
  79.1 0.7 copy.12
  79.9 0.7 copy.13
  80.6 0.7 copy.14
Async XLA Ops:
  0.6 0.7 copy-start.4
  0.6 0.7 copy-start.5
  1.3 0.9 %copy-start = (bf16[1,256,512]{2,1,0:T(8,128)(2,1)S(1)}, bf16[1,256,512]{2,1,0:T(8,128)(2,1)}, u32[]{:S(2)}) copy-start(bf16[1,256,512]{2,1,0:T(8,128)(2,1)} %param.6) | copy-start | bytes 786436
  2.3 0.9 %copy-start.1 = (bf16[1,256,512]{2,1,0:T(8,128)(2,1)S(1)}, bf16[1,256,512]{2,1,0:T(8,128)(2,1)}, u32[]{:S(2)}) copy-start(bf16[1,256,512]{2,1,0:T(8,128)(2,1)} %param.7) | copy-start | bytes 786436
  3.2 0.9 %copy-start.2 = (bf16[64,1536]{1,0:T(8,128)(2,1)S(1)}, bf16[64,1536]{1,0:T(8,128)(2,1)}, u32[]{:S(2)}) copy-start(bf16[64,1536]{1,0:T(8,128)(2,1)} %param.8) | copy-start | bytes 589828
  4.1 0.8 %copy-start.3 = (bf16[64,512]{1,0:T(8,128)(2,1)S(1)}, bf16[64,512]{1,0:T(8,128)(2,1)}, u32[]{:S(2)}) copy-start(bf16[64,512]{1,0:T(8,128)(2,1)} %param.9) | copy-start | bytes 196612

commit v3 on v2

--- a/solution.py
+++ b/solution.py
@@ -146,8 +146,8 @@
 
 
 def fused_kernel(peers, slot_rows, feats_hbm, grad_hbm, wq_hbm, wp_hbm, toh_hbm, toz_hbm,
-                 gf_ref, qg_ref, pg_ref,
-                 wf, wz_s, wz_r, wx_s, wx_r, wy_s, wy_r, wc_s, wc_r,
+                 gf_hbm, qg_hbm, pg_hbm,
+                 gf_ref, qg_ref, pg_ref, out_sem, wqf, wpf, wz_s, wz_r, wx_s, wx_r, wy_s, wy_r, wc_s, wc_r,
                  out_buf, arr_buf, sl_s, sl_r, back_buf, ret_buf, bk_s, bk_r,
                  fa, ft, ff_s, ff_r, q_v, k_v, v_v, g_v, h_v, at_v, dq_v, dk_v, dv_v,
                  dks, dkr, dk_s, dk_r, red_s, red_r, grad_v, toh, toz, in_sem, probs_v, *reds):
@@ -172,15 +172,21 @@
         sends.append(copy)
         return copy
 
-    wide = wq_hbm.shape[2]
     loads = []
     for i, (src, dst) in enumerate([(toh_hbm, toh), (toz_hbm, toz), (grad_hbm, grad_v),
-                                    (wq_hbm, wf.at[r, :, :, pl.ds(0, wide)]),
-                                    (wp_hbm, wf.at[r, :, :, pl.ds(wide, channels)]),
+                                    (wq_hbm, wqf.at[r]),
+                                    (wp_hbm, wpf.at[r]),
                                     (feats_hbm, fa.at[0])]):
         copy = pltpu.make_async_copy(src, dst, in_sem.at[i])
         copy.start()
         loads.append(copy)
+    handed = []
+
+    def hand(src, dst):
+        copy = pltpu.make_async_copy(src, dst, out_sem.at[len(handed)])
+        copy.start()
+        handed.append(copy)
+
     barrier = pltpu.get_barrier_semaphore()
     for k in range(1, peers):
         pl.semaphore_signal(barrier, inc=1, device_id=(lax.rem(r + k, peers), p), device_id_type=MESH)
@@ -203,48 +209,65 @@
         copy.wait()
     pl.semaphore_wait(barrier, peers - 1 + 3)
 
-    z_copies = []
-    for k in range(1, zs):
-        to = (lax.rem(z + k, zs) * 2 + x, p)
-        z_copies.append(send(wf.at[r, p], wf.at[r, p], wz_s.at[k - 1], wz_r.at[k - 1], to))
-    x_copies = [send(wf.at[r, p], wf.at[r, p], wx_s.at[0], wx_r.at[0], across_x)]
+    def wave(w, buf):
+        across_z, over_x, over_y, over_c = [], [], [], []
+
+        def go(flights, s_sem, r_sem, row, strip, device):
+            i = len(flights)
+            flights.append((send(buf.at[row, strip], buf.at[row, strip], s_sem.at[w, i], r_sem.at[w, i], device), row))
+
+        def start():
+            for k in range(1, zs):
+                go(across_z, wz_s, wz_r, r, p, (lax.rem(z + k, zs) * 2 + x, p))
+            go(over_x, wx_s, wx_r, r, p, across_x)
+
+        def after_z():
+            for k in range(1, zs):
+                across_z[k - 1][0].wait_recv()
+                row = lax.rem(z + zs - k, zs) * 2 + x
+                go(over_x, wx_s, wx_r, row, p, across_x)
+                go(over_y, wy_s, wy_r, row, p, across_y)
+                go(over_c, wc_s, wc_r, row, p, across_c)
+
+        def after_x():
+            for k in range(zs):
+                over_x[k][0].wait_recv()
+                row = lax.rem(z + zs - k, zs) * 2 + 1 - x
+                go(over_y, wy_s, wy_r, row, p, across_y)
+                go(over_c, wc_s, wc_r, row, p, across_c)
+
+        def after_y():
+            for copy, row in over_y:
+                copy.wait_recv()
+                go(over_c, wc_s, wc_r, row, p + 2 - 4 * y, across_c)
+
+        def finish():
+            for copy, _ in over_c:
+                copy.wait_recv()
+
+        return start, after_z, after_x, after_y, finish
+
+    start_q, after_z_q, after_x_q, after_y_q, finish_q = wave(0, wqf)
+    start_p, after_z_p, after_x_p, after_y_p, finish_p = wave(1, wpf)
+    start_q()
     f_copy = send(fa.at[0], fa.at[1], ff_s, ff_r, across_x)
-    y_copies, c_copies = [], []
-
-    def to_y(row):
-        i = len(y_copies)
-        y_copies.append((send(wf.at[row, p], wf.at[row, p], wy_s.at[i], wy_r.at[i], across_y), row))
-
-    def to_c(row, strip):
-        i = len(c_copies)
-        c_copies.append(send(wf.at[row, strip], wf.at[row, strip], wc_s.at[i], wc_r.at[i], across_c))
-
-    for k in range(1, zs):
-        z_copies[k - 1].wait_recv()
-        row = lax.rem(z + zs - k, zs) * 2 + x
-        x_copies.append(send(wf.at[row, p], wf.at[row, p], wx_s.at[k], wx_r.at[k], across_x))
-        to_y(row)
-        to_c(row, p)
+    after_z_q()
+    start_p()
     slot_copies = []
     for k in range(1, peers):
         d = lax.rem(r + k, peers)
         slot_copies.append(send(out_buf.at[d], arr_buf.at[r], sl_s.at[k - 1], sl_r.at[k - 1], (d, p)))
-    for k in range(zs):
-        x_copies[k].wait_recv()
-        row = lax.rem(z + zs - k, zs) * 2 + 1 - x
-        to_y(row)
-        to_c(row, p)
+    after_x_q()
     f_copy.wait_recv()
+    after_z_p()
     for i in range(2):
         ft[:, i * rows : (i + 1) * rows] = fa[i].astype(F32).T.astype(BF16)
-    for copy, row in y_copies:
-        copy.wait_recv()
-        to_c(row, p + 2 - 4 * y)
-    for copy in c_copies:
-        copy.wait_recv()
+    after_y_q()
+    after_x_p()
+    finish_q()
 
     def weight(lo, hi):
-        return wf[:, :, :, lo:hi].reshape(4 * STRIP * peers, hi - lo)
+        return wqf[:, :, :, lo:hi].reshape(4 * STRIP * peers, hi - lo)
 
     q_v[...] = dot(fa[0], weight(0, channels)).astype(BF16)
     for i in range(2):
@@ -318,6 +341,7 @@
                 qg_ref[:, lo : lo + PAIR] = value[:, i * PAIR : (i + 1) * PAIR]
         else:
             pg_ref[...] = value
+            hand(pg_ref, pg_hbm)
 
     stages = [stage1, stage2, stage3, stage4, stage5, stage6]
 
@@ -326,26 +350,39 @@
             if 0 <= t - i <= pairs:
                 stage(t - i)
 
-    for hp in range(pairs):
-        cols = slice(hp * PAIR, (hp + 1) * PAIR)
+    after_y_p()
+
+    def forward(hp, carry):
+        cols = pl.ds(pl.multiple_of(hp * PAIR, PAIR), PAIR)
         qp, kp = q_v[:, cols], k_v[:, cols]
         v_t = v_v[:, cols].astype(F32).T.astype(BF16)
+        parts = []
         for e in range(2):
-            mine = slice(e * head_size, (e + 1) * head_size)
             score = contract_cols(kp, qp * masks[e])
             raised = jnp.exp2((score - jnp.max(score, axis=0, keepdims=True)) * (scale * log2e))
             probs = raised * (1.0 / jnp.sum(raised, axis=0, keepdims=True))
             probs_v[2 * hp + e] = probs
-            at_v[hp * PAIR + e * head_size : hp * PAIR + (e + 1) * head_size, :] = dot(
-                v_t[mine], probs.astype(BF16)).astype(BF16)
-
+            parts.append(dot(v_t[e * head_size : (e + 1) * head_size], probs.astype(BF16)))
+        at_v[cols, :] = jnp.concatenate(parts, axis=0).astype(BF16)
+        return carry
+
+    lax.fori_loop(0, pairs, forward, 0)
+    finish_p()
     for copy in slot_copies:
         copy.wait_recv()
     place = jnp.where(slot_ids == rrow, 1.0, 0.0).astype(BF16)
     h_v[...] = contract_rows(place, arr_buf[...].reshape(slot_rows, channels)).astype(BF16)
     spread(0, 0, dot(at_v[...], h_v[...]))
     tick(0)
-    g_v[...] = contract_cols(h_v[...], weight(3 * channels, 4 * channels)).astype(BF16)
+    g_v[...] = contract_cols(h_v[...], wpf[...].reshape(4 * STRIP * peers, channels)).astype(BF16)
+
+    terms = []
+
+    def weight_terms(hp):
+        dq_b, dk_b, dv_b = terms[hp]
+        spread(1 + hp, 0, dot(ft[:, 0:rows], dq_b))
+        spread(1 + hp, PAIR, dot(ft[...], dk_b))
+        spread(1 + hp, 2 * PAIR, dot(ft[...], dv_b))
 
     dk_copies = []
     for hp in range(pairs):
@@ -375,10 +412,10 @@
         dq_v[:, cols] = dq_b
         dk_v[:, cols] = dk[:rows]
         dv_v[:, cols] = dv[:rows]
-        spread(1 + hp, 0, dot(ft[:, 0:rows], dq_b))
-        spread(1 + hp, PAIR, dot(ft[...], dk_b))
-        spread(1 + hp, 2 * PAIR, dot(ft[...], dv_b))
-        tick(1 + hp)
+        if hp > 0:
+            weight_terms(hp - 1)
+            tick(hp)
+        terms.append((dq_b, dk_b, dv_b))
     hfeat = contract_cols(dq_v[...], weight(0, channels))
     for lo, hi in ((0, pairs - 1), (pairs - 1, pairs)):
         part = slice(lo * PAIR, hi * PAIR)
@@ -396,16 +433,30 @@
     for k in range(1, peers):
         d = lax.rem(r + k, peers)
         back_copies.append(send(back_buf.at[d], ret_buf.at[r], bk_s.at[k - 1], bk_r.at[k - 1], (d, p)))
-    for t in range(pairs + 1, pairs + 4):
+    weight_terms(pairs - 1)
+    for t in range(pairs, pairs + 4):
         tick(t)
     for copy in back_copies:
         copy.wait_recv()
     pack = jnp.where(slot_ids == srow, 1.0, 0.0).astype(BF16)
     gf_ref[...] = contract_rows(pack, ret_buf[...].reshape(slot_rows, channels)).astype(BF16)
+    hand(gf_ref, gf_hbm)
     for t in range(pairs + 4, pairs + len(stages)):
         tick(t)
+    hand(qg_ref, qg_hbm)
     for copy in sends:
         copy.wait_send()
+    for copy in handed:
+        copy.wait()
+
+
+def hand_over(*refs):
+    count = len(refs) // 2
+    copies = [pltpu.make_async_copy(refs[i], refs[count + i], refs[-1].at[i]) for i in range(count)]
+    for copy in copies:
+        copy.start()
+    for copy in copies:
+        copy.wait()
 
 
 def per_device(feats, grad_out, qkv_weight, proj_weight, to_hilbert, to_zorder):
@@ -417,16 +468,17 @@
     slot_rows = peers * CAP * block
     zs = peers // 2
     pairs = channels // PAIR
-    wide = qkv_weight.shape[1] + channels
+    share, wide = qkv_weight.shape
     dma = pltpu.SemaphoreType.DMA
 
     def vm(*shape, kind=BF16):
         return pltpu.VMEM(shape, kind)
 
     scratch = [
-        vm(peers, 4, STRIP, wide),
-        dma((zs - 1,)), dma((zs - 1,)), dma((zs,)), dma((zs,)),
-        dma((peers - 1,)), dma((peers - 1,)), dma((2 * peers - 2,)), dma((2 * peers - 2,)),
+        vm(rows, channels), vm(share, wide, kind=F32), vm(share, channels, kind=F32), dma((3,)),
+        vm(peers, 4, STRIP, wide), vm(peers, 4, STRIP, channels),
+        dma((2, zs - 1)), dma((2, zs - 1)), dma((2, zs)), dma((2, zs)),
+        dma((2, peers - 1)), dma((2, peers - 1)), dma((2, 2 * peers - 2)), dma((2, 2 * peers - 2)),
         vm(peers, slot_rows // peers, channels), vm(peers, slot_rows // peers, channels),
         dma((peers - 1,)), dma((peers - 1,)),
         vm(peers, slot_rows // peers, channels), vm(peers, slot_rows // peers, channels),
@@ -448,21 +500,30 @@
     def body(*refs):
         fused_kernel(peers, slot_rows, *refs)
 
-    share = qkv_weight.shape[0]
-    grad_z, qkv_grad, proj_grad = pl.pallas_call(
+    shapes = (
+        jax.ShapeDtypeStruct((rows, channels), BF16),
+        jax.ShapeDtypeStruct((share, wide), F32),
+        jax.ShapeDtypeStruct((share, channels), F32),
+    )
+    hbm = pl.BlockSpec(memory_space=pltpu.HBM)
+    results = pl.pallas_call(
         body,
-        out_shape=(
-            jax.ShapeDtypeStruct((rows, channels), BF16),
-            jax.ShapeDtypeStruct((share, qkv_weight.shape[1]), F32),
-            jax.ShapeDtypeStruct((share, channels), F32),
-        ),
-        in_specs=[pl.BlockSpec(memory_space=pltpu.HBM)] * 6,
-        out_specs=(pl.BlockSpec(memory_space=pltpu.VMEM),) * 3,
+        out_shape=shapes,
+        in_specs=[hbm] * 6,
+        out_specs=(hbm,) * 3,
         scratch_shapes=scratch,
         compiler_params=pltpu.CompilerParams(
-            collective_id=0, has_side_effects=True, vmem_limit_bytes=48 * 1024 * 1024
+            collective_id=0, has_side_effects=True, vmem_limit_bytes=64 * 1024 * 1024
         ),
     )(feature, grad_out[0], qkv_weight.reshape(4, STRIP, -1), proj_weight.reshape(4, STRIP, -1), to_hilbert, to_zorder)
+    grad_z, qkv_grad, proj_grad = pl.pallas_call(
+        hand_over,
+        out_shape=shapes,
+        in_specs=[hbm] * 3,
+        out_specs=(hbm,) * 3,
+        scratch_shapes=[dma((3,))],
+        compiler_params=pltpu.CompilerParams(vmem_limit_bytes=64 * 1024 * 1024),
+    )(*results)
     return grad_z[None], qkv_grad, proj_grad
 
 

time: 81.5 us -> 100 us (1.23)
  Pallas kernels: 74.2 us -> 99.5 us
  local copies, waits for them, and re-layouts: 6.43 us -> 0 us
    pallas_call x1 -> x2, Pallas kernels: 74.2 us -> 99.5 us  [the longest x1 74.6 us: per_device(): pl.pallas_call(body, out_shape=shapes, in_specs=[hbm] * 6, out_specs=(hbm...]
    unnamed x15 -> x0, local copies, waits for them, and re-layouts: 6.43 us -> none
where the time goes in v3:
time: 100 us
  Pallas kernels  99.5 us (100%)
    pallas_call x1, Pallas kernels, per_device(): pl.pallas_call(body, out_shape=shapes, in_specs=[hbm] * 6, out_specs=(hbm...  74.6 us
    pallas_call x1, Pallas kernels, per_device(): pl.pallas_call(hand_over, out_shape=shapes, in_specs=[hbm] * 3, out_specs...  25 us

profile of v3, /device:TPU:0, one launch (start us, length us, event | category | flops | bytes accessed | tf_op | source)
XLA Modules:
  0.0 100.2 jit_solution(3853111511394485001)
XLA Ops:
  0.6 74.6 %shard_map.85 = (bf16[256,512]{1,0:T(8,128)(2,1)}, f32[64,1536]{1,0:T(8,128)}, f32[64,512]{1,0:T(8,128)}) custom-call(bf16[256,512]{1,0:T(8,128)(2,1)} %bitcast.5, bf16[256,512]{1,0:T(8,128)(2,1)} %bitcast.6, bf16[4,16,1536]{2,1,0:T(8,128)(2,1)} %bitcast.7, bf16[4,16,512]{2,1,0:T(8,128)(2,1)} %bitcast.8, s32[1,8]{1,0:T(1,128)} %refs_4_.1, s32[1,8]{1,0:T(1,128)} %refs_5_.1), custom_call_target="tpu_custom_call" | custom-call | tf_op jit(solution)/shard_map/pallas_call | solution.py:509
  75.2 25.0 %shard_map.86 = (bf16[256,512]{1,0:T(8,128)(2,1)}, f32[64,1536]{1,0:T(8,128)}, f32[64,512]{1,0:T(8,128)}) custom-call(bf16[256,512]{1,0:T(8,128)(2,1)} %get-tuple-element.9.refs_0_, f32[64,1536]{1,0:T(8,128)} %get-tuple-element.10.refs_1_, f32[64,512]{1,0:T(8,128)} %get-tuple-element.11.refs_2_), custom_call_target="tpu_custom_call" | custom-call | tf_op jit(solution)/shard_map/pallas_call | solution.py:519

commit v4 on v0

--- a/solution.py
+++ b/solution.py
@@ -1,6 +1,8 @@
 import jax
 import jax.numpy as jnp
 from jax import lax
+from jax.experimental import pallas as pl
+from jax.experimental.pallas import tpu as pltpu
 from jax.sharding import PartitionSpec as P
 
 HEADS = 8
@@ -39,7 +41,7 @@
     )
 
 
-def per_device(feats, grad_out, qkv_weight, proj_weight, to_hilbert, to_zorder):
+def per_device_general(feats, grad_out, qkv_weight, proj_weight, to_hilbert, to_zorder):
     peer_count = lax.axis_size("rows")
     feature = feats[0]
     rows_dev, channels = feature.shape
@@ -120,6 +122,433 @@
     return (grad_z[None], owned[:, : 3 * channels], owned[:, 3 * channels :])
 
 
+MESH = pl.DeviceIdType.MESH
+PAIR = 128
+STRIP = 16
+F32 = jnp.float32
+BF16 = jnp.bfloat16
+
+
+def dot(left, right):
+    return jnp.dot(left, right, preferred_element_type=F32)
+
+
+def slot_of_row(owners, order_keys, block, rows):
+    lane = lax.broadcasted_iota(jnp.int32, (1, rows), 1)
+    out = lax.rem(lane, block)
+    for i, owner in enumerate(owners):
+        rank = jnp.int32(0)
+        for j, other in enumerate(owners):
+            if j != i:
+                rank += jnp.where(jnp.logical_and(other == owner, order_keys[j] < order_keys[i]), 1, 0)
+        out += jnp.where(lax.div(lane, block) == i, (owner * CAP + rank) * block, 0)
+    return out
+
+
+def fused_kernel(peers, slot_rows, feats_hbm, grad_hbm, wq_hbm, wp_hbm, toh_hbm, toz_hbm,
+                 gf_hbm, qg_hbm, pg_hbm,
+                 gf_ref, qg_ref, pg_ref, out_sem, wf, wz_s, wz_r, wx_s, wx_r, wy_s, wy_r, wc_s, wc_r,
+                 out_buf, arr_buf, sl_s, sl_r, back_buf, ret_buf, bk_s, bk_r,
+                 fa, ft, ff_s, ff_r, q_v, k_v, v_v, h_v, at_v, dq_v, dk_v, dv_v, dkb_v, dvb_v, hf_v,
+                 dks, dkr, dk_s, dk_r, red_s, red_r, grad_v, toh, toz, in_sem, probs_v,
+                 term, r1, s1, r2, s2, r3, s3, r4, full):
+    rows, channels = feats_hbm.shape
+    blocks = toh_hbm.shape[1]
+    wide = wq_hbm.shape[2]
+    pairs = channels // PAIR
+    shard = 4 * STRIP
+    r = lax.axis_index("rows")
+    p = lax.axis_index("rep")
+    x, z = lax.rem(r, 2), lax.div(r, 2)
+    c, y = lax.rem(p, 2), lax.div(p, 2)
+    across_x = (r + 1 - 2 * x, p)
+    across_c = (r, p + 1 - 2 * c)
+    across_y = (r, p + 2 - 4 * y)
+    zs = peers // 2
+
+    def remote(src, dst, send_sem, recv_sem, device):
+        return pltpu.make_async_remote_copy(
+            src_ref=src, dst_ref=dst, send_sem=send_sem, recv_sem=recv_sem,
+            device_id=device, device_id_type=MESH)
+
+    def loop(lo, hi, body):
+        lax.fori_loop(lo, hi, lambda i, carry: (body(i), carry)[1], 0)
+
+    loads = []
+    for i, (src, dst) in enumerate([(toh_hbm, toh), (toz_hbm, toz), (grad_hbm, grad_v),
+                                    (wq_hbm, wf.at[r, :, :, pl.ds(0, wide)]),
+                                    (wp_hbm, wf.at[r, :, :, pl.ds(wide, channels)]),
+                                    (feats_hbm, fa.at[0])]):
+        copy = pltpu.make_async_copy(src, dst, in_sem.at[i])
+        copy.start()
+        loads.append(copy)
+
+    barrier = pltpu.get_barrier_semaphore()
+
+    def greet(device):
+        pl.semaphore_signal(barrier, inc=1, device_id=device, device_id_type=MESH)
+
+    loop(1, peers, lambda k: greet((lax.rem(r + k, peers), p)))
+    loop(1, 4, lambda k: greet((r, lax.rem(p + k, 4))))
+
+    for copy in loads[:2]:
+        copy.wait()
+    forward_list = [toh[0, i] for i in range(blocks)]
+    inverse_list = [toz[0, i] for i in range(blocks)]
+    srow = slot_of_row([lax.div(b, blocks) for b in forward_list], list(range(blocks)), rows // blocks, rows)
+    rrow = slot_of_row([lax.div(b, blocks) for b in inverse_list], inverse_list, rows // blocks, rows)
+    slot_ids = lax.broadcasted_iota(jnp.int32, (slot_rows, rows), 0)
+
+    def place(row):
+        return jnp.where(slot_ids == row, 1.0, 0.0).astype(BF16)
+
+    per_peer = slot_rows // peers
+    loads[2].wait()
+    out_buf[...] = dot(place(srow), grad_v[...]).astype(BF16).reshape(peers, per_peer, channels)
+    arr_buf[r] = out_buf[r]
+    for copy in loads[3:]:
+        copy.wait()
+    pl.semaphore_wait(barrier, peers - 1 + 3)
+
+    def row_of(j):
+        return lax.rem(z + zs - lax.rem(j, zs), zs) * 2 + lax.rem(x + lax.div(j, zs), 2)
+
+    def strip_copy(row, strip, s_sem, r_sem, i, device):
+        return remote(wf.at[row, strip], wf.at[row, strip], s_sem.at[i], r_sem.at[i], device)
+
+    def by_z(k):
+        return strip_copy(r, p, wz_s, wz_r, k - 1, (lax.rem(z + k, zs) * 2 + x, p))
+
+    def by_x(k):
+        return strip_copy(row_of(k), p, wx_s, wx_r, k, across_x)
+
+    def by_y(j):
+        return strip_copy(row_of(j), p, wy_s, wy_r, j - 1, across_y)
+
+    def by_c(j):
+        return strip_copy(row_of(j), p, wc_s, wc_r, j - 1, across_c)
+
+    def by_yc(j):
+        return strip_copy(row_of(j), p + 2 - 4 * y, wc_s, wc_r, peers - 2 + j, across_c)
+
+    def slot_copy(k):
+        d = lax.rem(r + k, peers)
+        return remote(out_buf.at[d], arr_buf.at[r], sl_s.at[k - 1], sl_r.at[k - 1], (d, p))
+
+    def back_copy(k):
+        d = lax.rem(r + k, peers)
+        return remote(back_buf.at[d], ret_buf.at[r], bk_s.at[k - 1], bk_r.at[k - 1], (d, p))
+
+    feats_copy = remote(fa.at[0], fa.at[1], ff_s, ff_r, across_x)
+
+    loop(1, zs, lambda k: by_z(k).start())
+    by_x(0).start()
+    feats_copy.start()
+
+    def after_z(k):
+        by_z(k).wait_recv()
+        by_x(k).start()
+        by_y(k).start()
+        by_c(k).start()
+
+    def after_x(k):
+        by_x(k).wait_recv()
+        by_y(zs + k).start()
+        by_c(zs + k).start()
+
+    def after_y(j):
+        by_y(j).wait_recv()
+        by_yc(j).start()
+
+    def after_c(j):
+        by_c(j).wait_recv()
+        by_yc(j).wait_recv()
+
+    loop(1, zs, after_z)
+    loop(1, peers, lambda k: slot_copy(k).start())
+    loop(0, zs, after_x)
+    feats_copy.wait_recv()
+
+    def turn(i):
+        ft[:, pl.ds(pl.multiple_of(i * rows, rows), rows)] = fa[i].astype(F32).T.astype(BF16)
+
+    loop(0, 2, turn)
+    loop(1, peers, after_y)
+    loop(1, peers, after_c)
+
+    def pair_cols(hp, base=0):
+        return pl.ds(pl.multiple_of(base + hp * PAIR, PAIR), PAIR)
+
+    def weight(i, hp):
+        return wf[:, :, :, pair_cols(hp, i * channels)].reshape(shard * peers, PAIR)
+
+    head_size = channels // HEADS
+    scale = head_size ** (-0.5)
+    log2e = 1.4426950408889634
+    lane = lax.broadcasted_iota(jnp.int32, (1, PAIR), 1)
+    masks = [jnp.where(lane < head_size, 1.0, 0.0).astype(BF16), jnp.where(lane < head_size, 0.0, 1.0).astype(BF16)]
+
+    def forward(hp):
+        cols = pair_cols(hp)
+        both = fa[...].reshape(2 * rows, channels)
+        qp = dot(fa[0], weight(0, hp)).astype(BF16)
+        kp = dot(both, weight(1, hp)).astype(BF16)
+        vp = dot(both, weight(2, hp)).astype(BF16)
+        q_v[:, cols], k_v[:, cols], v_v[:, cols] = qp, kp, vp
+        v_t = vp.astype(F32).T.astype(BF16)
+        parts = []
+        for e in range(2):
+            score = contract_cols(kp, qp * masks[e])
+            raised = jnp.exp2((score - jnp.max(score, axis=0, keepdims=True)) * (scale * log2e))
+            probs = raised * (1.0 / jnp.sum(raised, axis=0, keepdims=True))
+            probs_v[2 * hp + e] = probs
+            parts.append(dot(v_t[e * head_size : (e + 1) * head_size], probs.astype(BF16)))
+        at_v[cols, :] = jnp.concatenate(parts, axis=0).astype(BF16)
+
+    loop(0, pairs, forward)
+    loop(1, peers, lambda k: slot_copy(k).wait_recv())
+    h_v[...] = contract_rows(place(rrow), arr_buf[...].reshape(slot_rows, channels)).astype(BF16)
+    hf_v[...] = jnp.zeros_like(hf_v)
+
+    def dk_copy(hp):
+        return remote(dks.at[hp], dkr.at[hp], dk_s.at[hp], dk_r.at[hp], across_x)
+
+    def backward(hp):
+        cols = pair_cols(hp)
+        qp, kp, vp = q_v[:, cols], k_v[:, cols], v_v[:, cols]
+        w_rows = wf[pl.ds(hp * (PAIR // shard), PAIR // shard), :, :, wide:].reshape(PAIR, channels)
+        gp = contract_cols(h_v[...], w_rows).astype(BF16)
+        k_t = kp.astype(F32).T.astype(BF16)
+        dk = dv = None
+        dq_t = []
+        for e in range(2):
+            mine = slice(e * head_size, (e + 1) * head_size)
+            qm, gm = qp * masks[e], gp * masks[e]
+            probs = probs_v[2 * hp + e]
+            probs_b = probs.astype(BF16)
+            dprob = contract_cols(vp, gm)
+            delta = jnp.sum(probs * dprob, axis=0, keepdims=True)
+            dscore = (probs * (dprob - delta)).astype(BF16)
+            dq_t.append(dot(k_t[mine], dscore))
+            dk_e, dv_e = dot(dscore, qm), dot(probs_b, gm)
+            dk = dk_e if dk is None else dk + dk_e
+            dv = dv_e if dv is None else dv + dv_e
+        dk = dk * scale
+        dk_b, dv_b = dk.astype(BF16), dv.astype(BF16)
+        dks[hp, 0] = dk_b[rows:]
+        dks[hp, 1] = dv_b[rows:]
+        dk_copy(hp).start()
+        dq_v[:, cols] = (jnp.concatenate(dq_t, axis=0) * scale).T.astype(BF16)
+        dk_v[:, cols], dv_v[:, cols] = dk[:rows], dv[:rows]
+        dkb_v[:, cols], dvb_v[:, cols] = dk_b, dv_b
+
+    def add_hfeat(hp):
+        cols = pair_cols(hp)
+        dk_copy(hp).wait_recv()
+        dk = (dk_v[:, cols] + dkr[hp, 0].astype(F32)).astype(BF16)
+        dv = (dv_v[:, cols] + dkr[hp, 1].astype(F32)).astype(BF16)
+        left = jnp.concatenate([dq_v[:, cols], dk, dv], axis=1)
+        right = jnp.concatenate([weight(i, hp) for i in range(3)], axis=1)
+        hf_v[...] += contract_cols(left, right)
+
+    def go_back():
+        back_buf[...] = dot(place(rrow), hf_v[...].astype(BF16)).astype(BF16).reshape(peers, per_peer, channels)
+        ret_buf[r] = back_buf[r]
+        loop(1, peers, lambda k: back_copy(k).start())
+
+    def red(ch, i, src, dst, device):
+        return remote(src, dst, red_s.at[ch, i], red_r.at[ch, i], device)
+
+    def red1(ch):
+        return red(ch, 0, term.at[ch, 1 - c], r1.at[ch], across_c)
+
+    def red2(ch):
+        return red(ch, 1, s1.at[ch, 1 - y], r2.at[ch], across_y)
+
+    def red3(ch):
+        return red(ch, 2, s2.at[ch, 1 - x], r3.at[ch], across_x)
+
+    def red4(ch, k):
+        zz = lax.rem(z + k, zs)
+        return red(ch, 2 + k, s3.at[ch, zz], r4.at[ch, k - 1], (zz * 2 + x, p))
+
+    def red5(ch, k):
+        return red(ch, 1 + zs + k, full.at[ch, p], full.at[ch, p], (r, lax.rem(p + k, 4)))
+
+    def stage1(ch):
+        cols = pair_cols(ch)
+        parts = [dot(ft[:, 0:rows], dq_v[:, cols]), dot(ft[...], dkb_v[:, cols]), dot(ft[...], dvb_v[:, cols]),
+                 dot(at_v[...], h_v[:, cols])]
+        for j, part in enumerate(parts):
+            part = part.astype(BF16)
+            for i in range(4 * peers):
+                cc, yy, xx, zz = i % 2, i // 2 % 2, i // 4 % 2, i // 8
+                term[ch, cc, yy, xx, zz, :, j * PAIR : (j + 1) * PAIR] = part[i * STRIP : (i + 1) * STRIP, :]
+        red1(ch).start()
+
+    def stage2(ch):
+        red1(ch).wait_recv()
+        s1[ch] = (term[ch, c].astype(F32) + r1[ch].astype(F32)).astype(BF16)
+        red2(ch).start()
+
+    def stage3(ch):
+        red2(ch).wait_recv()
+        s2[ch] = (s1[ch, y].astype(F32) + r2[ch].astype(F32)).astype(BF16)
+        red3(ch).start()
+
+    def stage4(ch):
+        red3(ch).wait_recv()
+        s3[ch] = (s2[ch, x].astype(F32) + r3[ch].astype(F32)).astype(BF16)
+        for k in range(1, zs):
+            red4(ch, k).start()
+
+    def stage5(ch):
+        total = s3[ch, z].astype(F32)
+        for k in range(1, zs):
+            red4(ch, k).wait_recv()
+            total = total + r4[ch, k - 1].astype(F32)
+        full[ch, p] = total.astype(BF16)
+        for k in range(1, 4):
+            red5(ch, k).start()
+
+    def stage6(ch):
+        for k in range(1, 4):
+            red5(ch, k).wait_recv()
+        value = full[ch].astype(F32).reshape(shard, 4 * PAIR)
+        for i in range(3):
+            qg_ref[:, pair_cols(ch, i * channels)] = value[:, i * PAIR : (i + 1) * PAIR]
+        pg_ref[:, pair_cols(ch)] = value[:, 3 * PAIR :]
+
+    stages = [stage1, stage2, stage3, stage4, stage5, stage6]
+
+    def tick(t):
+        pl.when(t < pairs)(lambda: backward(t))
+        pl.when(jnp.logical_and(t >= 1, t <= pairs))(lambda: add_hfeat(t - 1))
+        pl.when(t == pairs)(go_back)
+        for i, stage in enumerate(stages):
+            pl.when(jnp.logical_and(t >= i + 1, t < i + 1 + pairs))(lambda stage=stage, i=i: stage(t - i - 1))
+
+    loop(0, pairs + len(stages), tick)
+    outs = [pltpu.make_async_copy(src, dst, out_sem.at[i])
+            for i, (src, dst) in enumerate([(qg_ref, qg_hbm), (pg_ref, pg_hbm), (gf_ref, gf_hbm)])]
+    outs[0].start()
+    outs[1].start()
+    loop(1, peers, lambda k: back_copy(k).wait_recv())
+    gf_ref[...] = contract_rows(place(srow), ret_buf[...].reshape(slot_rows, channels)).astype(BF16)
+    outs[2].start()
+
+    def sent_rows(k):
+        slot_copy(k).wait_send()
+        back_copy(k).wait_send()
+        by_y(k).wait_send()
+        by_c(k).wait_send()
+        by_yc(k).wait_send()
+
+    def sent_chunk(ch):
+        dk_copy(ch).wait_send()
+        for one in (red1, red2, red3):
+            one(ch).wait_send()
+        for k in range(1, zs):
+            red4(ch, k).wait_send()
+        for k in range(1, 4):
+            red5(ch, k).wait_send()
+
+    loop(1, zs, lambda k: by_z(k).wait_send())
+    loop(0, zs, lambda k: by_x(k).wait_send())
+    feats_copy.wait_send()
+    loop(1, peers, sent_rows)
+    loop(0, pairs, sent_chunk)
+    for copy in outs:
+        copy.wait()
+
+
+def hand_over(*refs):
+    count = (len(refs) - 2) // 3
+    ins, outs, held = refs[:count], refs[count : 2 * count], refs[2 * count : 3 * count]
+    first = [pltpu.make_async_copy(ins[i], held[i], refs[-2].at[i]) for i in range(count)]
+    second = [pltpu.make_async_copy(held[i], outs[i], refs[-1].at[i]) for i in range(count)]
+    for copy in first:
+        copy.start()
+    for i in range(count):
+        first[i].wait()
+        second[i].start()
+    for copy in second:
+        copy.wait()
+
+
+def per_device(feats, grad_out, qkv_weight, proj_weight, to_hilbert, to_zorder):
+    peers = lax.axis_size("rows")
+    feature = feats[0]
+    rows, channels = feature.shape
+    blocks = to_hilbert.shape[1]
+    block = rows // blocks
+    slot_rows = peers * CAP * block
+    zs = peers // 2
+    pairs = channels // PAIR
+    share, wide = qkv_weight.shape
+    dma = pltpu.SemaphoreType.DMA
+
+    def vm(*shape, kind=BF16):
+        return pltpu.VMEM(shape, kind)
+
+    width = 4 * PAIR
+    scratch = [
+        vm(rows, channels), vm(share, wide, kind=F32), vm(share, channels, kind=F32), dma((3,)),
+        vm(peers, 4, STRIP, wide + channels),
+        dma((zs - 1,)), dma((zs - 1,)), dma((zs,)), dma((zs,)),
+        dma((peers - 1,)), dma((peers - 1,)), dma((2 * peers - 2,)), dma((2 * peers - 2,)),
+        vm(peers, slot_rows // peers, channels), vm(peers, slot_rows // peers, channels),
+        dma((peers - 1,)), dma((peers - 1,)),
+        vm(peers, slot_rows // peers, channels), vm(peers, slot_rows // peers, channels),
+        dma((peers - 1,)), dma((peers - 1,)),
+        vm(2, rows, channels), vm(channels, 2 * rows), dma, dma,
+        vm(rows, channels), vm(2 * rows, channels), vm(2 * rows, channels), vm(rows, channels),
+        vm(channels, rows), vm(rows, channels), vm(rows, channels, kind=F32), vm(rows, channels, kind=F32),
+        vm(2 * rows, channels), vm(2 * rows, channels), vm(rows, channels, kind=F32),
+        vm(pairs, 2, rows, PAIR), vm(pairs, 2, rows, PAIR), dma((pairs,)), dma((pairs,)),
+        dma((pairs, zs + 5)), dma((pairs, zs + 5)),
+        vm(rows, channels), pltpu.SMEM((1, blocks), jnp.int32), pltpu.SMEM((1, blocks), jnp.int32), dma((6,)),
+        vm(HEADS, 2 * rows, rows, kind=F32),
+        vm(pairs, 2, 2, 2, zs, STRIP, width), vm(pairs, 2, 2, zs, STRIP, width), vm(pairs, 2, 2, zs, STRIP, width),
+        vm(pairs, 2, zs, STRIP, width), vm(pairs, 2, zs, STRIP, width),
+        vm(pairs, zs, STRIP, width), vm(pairs, zs, STRIP, width),
+        vm(pairs, zs - 1, STRIP, width), vm(pairs, 4, STRIP, width),
+    ]
+
+    def body(*refs):
+        fused_kernel(peers, slot_rows, *refs)
+
+    shapes = (
+        jax.ShapeDtypeStruct((rows, channels), BF16),
+        jax.ShapeDtypeStruct((share, wide), F32),
+        jax.ShapeDtypeStruct((share, channels), F32),
+    )
+    hbm = pl.BlockSpec(memory_space=pltpu.HBM)
+    results = pl.pallas_call(
+        body,
+        out_shape=shapes,
+        in_specs=[hbm] * 6,
+        out_specs=(hbm,) * 3,
+        scratch_shapes=scratch,
+        compiler_params=pltpu.CompilerParams(
+            collective_id=0, has_side_effects=True, vmem_limit_bytes=64 * 1024 * 1024
+        ),
+    )(feature, grad_out[0], qkv_weight.reshape(4, STRIP, -1), proj_weight.reshape(4, STRIP, -1), to_hilbert, to_zorder)
+    grad_z, qkv_grad, proj_grad = pl.pallas_call(
+        hand_over,
+        out_shape=shapes,
+        in_specs=[hbm] * 3,
+        out_specs=(hbm,) * 3,
+        scratch_shapes=[pltpu.VMEM(one.shape, one.dtype) for one in shapes] + [dma((3,)), dma((3,))],
+        compiler_params=pltpu.CompilerParams(vmem_limit_bytes=64 * 1024 * 1024),
+    )(*results)
+    return grad_z[None], qkv_grad, proj_grad
+
+
+def fits_kernel(mesh):
+    return mesh.shape["rows"] == 8 and mesh.shape["rep"] == 4
+
+
 def solution(mesh):
     placed = (
         P("rep", "rows", None),
@@ -130,7 +559,7 @@
         P("rep", "rows"),
     )
     return jax.shard_map(
-        per_device,
+        per_device if fits_kernel(mesh) else per_device_general,
         mesh=mesh,
         in_specs=placed,
         out_specs=(P("rep", "rows", None), P("rows", None), P("rows", None)),

time: 313 us -> 80.1 us (0.26)
  waiting for transfers between devices: 160 us -> 0 us
  Pallas kernels: 0 us -> 79.3 us
  matrix products: 49.1 us -> 0 us
  blocking collectives: 45.5 us -> 0 us
  local copies, waits for them, and re-layouts: 16.5 us -> 0 us
  starting transfers between devices: 15.1 us -> 0 us
  between operations: 14.9 us -> 0.64 us
  other arithmetic: 11.5 us -> 0 us
    psum x1 -> x0, waiting for transfers between devices: 121 us -> none  [per_device(): total = lax.psum(term, ('rows', 'rep'))]
    pallas_call x0 -> x2, Pallas kernels: none -> 79.3 us  [the longest x1 77.4 us: per_device(): pl.pallas_call(body, out_shape=shapes, in_specs=[hbm] * 6, out_specs=(hbm...]
    dot_general x57 -> x0, matrix products: 49.1 us -> none  [the longest x18 25.6 us: contract_cols(): lax.dot_general(left, right, (((1,), (1,)), ((), ())), preferred_element_...]
    all_gather x1 -> x0, blocking collectives: 45.5 us -> none  [per_device(): lax.all_gather(proj_weight, 'rows', axis=0, tiled=True)]
    all_to_all x2 -> x0, waiting for transfers between devices: 19.2 us -> none  [move_blocks(): lax.all_to_all(outgoing, 'rows', split_axis=0, concat_axis=0, tiled=True)]
    ppermute x3 -> x0, waiting for transfers between devices: 17.6 us -> none  [from_partner(): return lax.ppermute(block, axis, route)]
    all_to_all x2 -> x0, starting transfers between devices: 10.7 us -> none  [move_blocks(): lax.all_to_all(outgoing, 'rows', split_axis=0, concat_axis=0, tiled=True)]
    unnamed x106 -> x0, local copies, waits for them, and re-layouts: 5.42 us -> none
  transfers between devices with their start and end apart: 7 -> 0, of which waited for: 5 -> 0; matrix products, arithmetic and copies ran while one was open for 7% -> 0% of each run, Pallas kernels for 0% -> 0%
where the time goes in v4:
time: 80.1 us; the launch traced here: 80 us
  Pallas kernels  79.3 us (99%)
    pallas_call x1, Pallas kernels, per_device(): pl.pallas_call(body, out_shape=shapes, in_specs=[hbm] * 6, out_specs=(hbm...  77.4 us
    pallas_call x1, Pallas kernels, per_device(): pl.pallas_call(hand_over, out_shape=shapes, in_specs=[hbm] * 3, out_specs...  1.91 us

profile of v4, /device:TPU:0, one launch (start us, length us, event | category | flops | bytes accessed | tf_op | source)
XLA Modules:
  0.0 80.0 jit_solution(12907902145853955369)
XLA Ops:
  0.6 77.4 %shard_map.85 = (bf16[256,512]{1,0:T(8,128)(2,1)}, f32[64,1536]{1,0:T(8,128)}, f32[64,512]{1,0:T(8,128)}) custom-call(bf16[256,512]{1,0:T(8,128)(2,1)} %bitcast.5, bf16[256,512]{1,0:T(8,128)(2,1)} %bitcast.6, bf16[4,16,1536]{2,1,0:T(8,128)(2,1)} %bitcast.7, bf16[4,16,512]{2,1,0:T(8,128)(2,1)} %bitcast.8, s32[1,8]{1,0:T(1,128)} %refs_4_.1, s32[1,8]{1,0:T(1,128)} %refs_5_.1), custom_call_target="tpu_custom_call" | custom-call | tf_op jit(solution)/shard_map/pallas_call | solution.py:527
  78.0 1.9 %shard_map.86 = (bf16[256,512]{1,0:T(8,128)(2,1)}, f32[64,1536]{1,0:T(8,128)}, f32[64,512]{1,0:T(8,128)}) custom-call(bf16[256,512]{1,0:T(8,128)(2,1)} %get-tuple-element.9.refs_0_, f32[64,1536]{1,0:T(8,128)} %get-tuple-element.10.refs_1_, f32[64,512]{1,0:T(8,128)} %get-tuple-element.11.refs_2_), custom_call_target="tpu_custom_call" | custom-call | tf_op jit(solution)/shard_map/pallas_call | solution.py:537

commit v5 on v4

--- a/solution.py
+++ b/solution.py
@@ -191,6 +191,48 @@
     loop(1, peers, lambda k: greet((lax.rem(r + k, peers), p)))
     loop(1, 4, lambda k: greet((r, lax.rem(p + k, 4))))
 
+
+    def place(row):
+        return jnp.where(slot_ids == row, 1.0, 0.0).astype(BF16)
+
+    per_peer = slot_rows // peers
+    for copy in loads[3:5]:
+        copy.wait()
+    pl.semaphore_wait(barrier, peers - 1 + 3)
+
+    def row_of(j):
+        return lax.rem(z + zs - lax.rem(j, zs), zs) * 2 + lax.rem(x + lax.div(j, zs), 2)
+
+    def strip_copy(row, strip, s_sem, r_sem, i, device):
+        return remote(wf.at[row, strip], wf.at[row, strip], s_sem.at[i], r_sem.at[i], device)
+
+    def by_z(k):
+        return strip_copy(r, p, wz_s, wz_r, k - 1, (lax.rem(z + k, zs) * 2 + x, p))
+
+    def by_x(k):
+        return strip_copy(row_of(k), p, wx_s, wx_r, k, across_x)
+
+    def by_y(j):
+        return strip_copy(row_of(j), p, wy_s, wy_r, j - 1, across_y)
+
+    def by_c(j):
+        return strip_copy(row_of(j), p, wc_s, wc_r, j - 1, across_c)
+
+    def by_yc(j):
+        return strip_copy(row_of(j), p + 2 - 4 * y, wc_s, wc_r, peers - 2 + j, across_c)
+
+    def slot_copy(k):
+        d = lax.rem(r + k, peers)
+        return remote(out_buf.at[d], arr_buf.at[r], sl_s.at[k - 1], sl_r.at[k - 1], (d, p))
+
+    def back_copy(k):
+        d = lax.rem(r + k, peers)
+        return remote(back_buf.at[d], ret_buf.at[r], bk_s.at[k - 1], bk_r.at[k - 1], (d, p))
+
+    feats_copy = remote(fa.at[0], fa.at[1], ff_s, ff_r, across_x)
+
+    loop(1, zs, lambda k: by_z(k).start())
+    by_x(0).start()
     for copy in loads[:2]:
         copy.wait()
     forward_list = [toh[0, i] for i in range(blocks)]
@@ -198,52 +240,9 @@
     srow = slot_of_row([lax.div(b, blocks) for b in forward_list], list(range(blocks)), rows // blocks, rows)
     rrow = slot_of_row([lax.div(b, blocks) for b in inverse_list], inverse_list, rows // blocks, rows)
     slot_ids = lax.broadcasted_iota(jnp.int32, (slot_rows, rows), 0)
-
-    def place(row):
-        return jnp.where(slot_ids == row, 1.0, 0.0).astype(BF16)
-
-    per_peer = slot_rows // peers
     loads[2].wait()
     out_buf[...] = dot(place(srow), grad_v[...]).astype(BF16).reshape(peers, per_peer, channels)
     arr_buf[r] = out_buf[r]
-    for copy in loads[3:]:
-        copy.wait()
-    pl.semaphore_wait(barrier, peers - 1 + 3)
-
-    def row_of(j):
-        return lax.rem(z + zs - lax.rem(j, zs), zs) * 2 + lax.rem(x + lax.div(j, zs), 2)
-
-    def strip_copy(row, strip, s_sem, r_sem, i, device):
-        return remote(wf.at[row, strip], wf.at[row, strip], s_sem.at[i], r_sem.at[i], device)
-
-    def by_z(k):
-        return strip_copy(r, p, wz_s, wz_r, k - 1, (lax.rem(z + k, zs) * 2 + x, p))
-
-    def by_x(k):
-        return strip_copy(row_of(k), p, wx_s, wx_r, k, across_x)
-
-    def by_y(j):
-        return strip_copy(row_of(j), p, wy_s, wy_r, j - 1, across_y)
-
-    def by_c(j):
-        return strip_copy(row_of(j), p, wc_s, wc_r, j - 1, across_c)
-
-    def by_yc(j):
-        return strip_copy(row_of(j), p + 2 - 4 * y, wc_s, wc_r, peers - 2 + j, across_c)
-
-    def slot_copy(k):
-        d = lax.rem(r + k, peers)
-        return remote(out_buf.at[d], arr_buf.at[r], sl_s.at[k - 1], sl_r.at[k - 1], (d, p))
-
-    def back_copy(k):
-        d = lax.rem(r + k, peers)
-        return remote(back_buf.at[d], ret_buf.at[r], bk_s.at[k - 1], bk_r.at[k - 1], (d, p))
-
-    feats_copy = remote(fa.at[0], fa.at[1], ff_s, ff_r, across_x)
-
-    loop(1, zs, lambda k: by_z(k).start())
-    by_x(0).start()
-    feats_copy.start()
 
     def after_z(k):
         by_z(k).wait_recv()
@@ -265,8 +264,10 @@
         by_yc(j).wait_recv()
 
     loop(1, zs, after_z)
+    loads[5].wait()
+    feats_copy.start()
+    loop(0, zs, after_x)
     loop(1, peers, lambda k: slot_copy(k).start())
-    loop(0, zs, after_x)
     feats_copy.wait_recv()
 
     def turn(i):
@@ -419,7 +420,7 @@
             qg_ref[:, pair_cols(ch, i * channels)] = value[:, i * PAIR : (i + 1) * PAIR]
         pg_ref[:, pair_cols(ch)] = value[:, 3 * PAIR :]
 
-    stages = [stage1, stage2, stage3, stage4, stage5, stage6]
+    stages = [stage1, stage2, stage3, stage4]
 
     def tick(t):
         pl.when(t < pairs)(lambda: backward(t))
@@ -429,12 +430,14 @@
             pl.when(jnp.logical_and(t >= i + 1, t < i + 1 + pairs))(lambda stage=stage, i=i: stage(t - i - 1))
 
     loop(0, pairs + len(stages), tick)
-    outs = [pltpu.make_async_copy(src, dst, out_sem.at[i])
-            for i, (src, dst) in enumerate([(qg_ref, qg_hbm), (pg_ref, pg_hbm), (gf_ref, gf_hbm)])]
-    outs[0].start()
-    outs[1].start()
+    loop(0, pairs, stage5)
     loop(1, peers, lambda k: back_copy(k).wait_recv())
     gf_ref[...] = contract_rows(place(srow), ret_buf[...].reshape(slot_rows, channels)).astype(BF16)
+    outs = [pltpu.make_async_copy(src, dst, out_sem.at[i])
+            for i, (src, dst) in enumerate([(gf_ref, gf_hbm), (qg_ref, qg_hbm), (pg_ref, pg_hbm)])]
+    outs[0].start()
+    loop(0, pairs, stage6)
+    outs[1].start()
     outs[2].start()
 
     def sent_rows(k):

time: 80.1 us -> 75.1 us (0.938)
  Pallas kernels: 79.3 us -> 74.3 us
    pallas_call x1, Pallas kernels: 77.4 us -> 72.4 us  [per_device(): pl.pallas_call(body, out_shape=shapes, in_specs=[hbm] * 6, out_specs=(hbm...]
where the time goes in v5:
time: 75.1 us; the launch traced here: 75 us
  Pallas kernels  74.3 us (99%)
    pallas_call x1, Pallas kernels, per_device(): pl.pallas_call(body, out_shape=shapes, in_specs=[hbm] * 6, out_specs=(hbm...  72.4 us
    pallas_call x1, Pallas kernels, per_device(): pl.pallas_call(hand_over, out_shape=shapes, in_specs=[hbm] * 3, out_specs...  1.91 us

profile of v5, /device:TPU:0, one launch (start us, length us, event | category | flops | bytes accessed | tf_op | source)
XLA Modules:
  0.0 75.0 jit_solution(9968631373177211856)
XLA Ops:
  0.6 72.4 %shard_map.85 = (bf16[256,512]{1,0:T(8,128)(2,1)}, f32[64,1536]{1,0:T(8,128)}, f32[64,512]{1,0:T(8,128)}) custom-call(bf16[256,512]{1,0:T(8,128)(2,1)} %bitcast.5, bf16[256,512]{1,0:T(8,128)(2,1)} %bitcast.6, bf16[4,16,1536]{2,1,0:T(8,128)(2,1)} %bitcast.7, bf16[4,16,512]{2,1,0:T(8,128)(2,1)} %bitcast.8, s32[1,8]{1,0:T(1,128)} %refs_4_.1, s32[1,8]{1,0:T(1,128)} %refs_5_.1), custom_call_target="tpu_custom_call" | custom-call | tf_op jit(solution)/shard_map/pallas_call | solution.py:530
  73.1 1.9 %shard_map.86 = (bf16[256,512]{1,0:T(8,128)(2,1)}, f32[64,1536]{1,0:T(8,128)}, f32[64,512]{1,0:T(8,128)}) custom-call(bf16[256,512]{1,0:T(8,128)(2,1)} %get-tuple-element.9.refs_0_, f32[64,1536]{1,0:T(8,128)} %get-tuple-element.10.refs_1_, f32[64,512]{1,0:T(8,128)} %get-tuple-element.11.refs_2_), custom_call_target="tpu_custom_call" | custom-call | tf_op jit(solution)/shard_map/pallas_call | solution.py:540

commit v6 on v5

--- a/solution.py
+++ b/solution.py
@@ -157,6 +157,7 @@
     wide = wq_hbm.shape[2]
     pairs = channels // PAIR
     shard = 4 * STRIP
+    half = channels // 2
     r = lax.axis_index("rows")
     p = lax.axis_index("rep")
     x, z = lax.rem(r, 2), lax.div(r, 2)
@@ -176,9 +177,11 @@
 
     loads = []
     for i, (src, dst) in enumerate([(toh_hbm, toh), (toz_hbm, toz), (grad_hbm, grad_v),
-                                    (wq_hbm, wf.at[r, :, :, pl.ds(0, wide)]),
-                                    (wp_hbm, wf.at[r, :, :, pl.ds(wide, channels)]),
-                                    (feats_hbm, fa.at[0])]):
+                                    (wp_hbm, wf.at[1, r, :, :, pl.ds(wide // 2, channels)]),
+                                    (feats_hbm, fa.at[0])]
+                                   + [(wq_hbm.at[:, :, pl.ds(j * channels + w * half, half)],
+                                       wf.at[w, r, :, :, pl.ds(j * half, half)])
+                                      for w in range(2) for j in range(3)]):
         copy = pltpu.make_async_copy(src, dst, in_sem.at[i])
         copy.start()
         loads.append(copy)
@@ -196,30 +199,77 @@
         return jnp.where(slot_ids == row, 1.0, 0.0).astype(BF16)
 
     per_peer = slot_rows // peers
-    for copy in loads[3:5]:
+    for copy in [loads[3]] + loads[5:]:
         copy.wait()
     pl.semaphore_wait(barrier, peers - 1 + 3)
 
     def row_of(j):
         return lax.rem(z + zs - lax.rem(j, zs), zs) * 2 + lax.rem(x + lax.div(j, zs), 2)
 
-    def strip_copy(row, strip, s_sem, r_sem, i, device):
-        return remote(wf.at[row, strip], wf.at[row, strip], s_sem.at[i], r_sem.at[i], device)
-
-    def by_z(k):
-        return strip_copy(r, p, wz_s, wz_r, k - 1, (lax.rem(z + k, zs) * 2 + x, p))
-
-    def by_x(k):
-        return strip_copy(row_of(k), p, wx_s, wx_r, k, across_x)
-
-    def by_y(j):
-        return strip_copy(row_of(j), p, wy_s, wy_r, j - 1, across_y)
-
-    def by_c(j):
-        return strip_copy(row_of(j), p, wc_s, wc_r, j - 1, across_c)
-
-    def by_yc(j):
-        return strip_copy(row_of(j), p + 2 - 4 * y, wc_s, wc_r, peers - 2 + j, across_c)
+    class Wave:
+        def __init__(self, w):
+            self.w, self.cols = w, pl.ds(0, wide // 2 if w == 0 else wide // 2 + channels)
+
+        def strip_copy(self, row, strip, s_sem, r_sem, i, device):
+            ref = wf.at[self.w, row, strip, :, self.cols]
+            return remote(ref, ref, s_sem.at[self.w, i], r_sem.at[self.w, i], device)
+
+        def by_z(self, k):
+            return self.strip_copy(r, p, wz_s, wz_r, k - 1, (lax.rem(z + k, zs) * 2 + x, p))
+
+        def by_x(self, k):
+            return self.strip_copy(row_of(k), p, wx_s, wx_r, k, across_x)
+
+        def by_y(self, j):
+            return self.strip_copy(row_of(j), p, wy_s, wy_r, j - 1, across_y)
+
+        def by_c(self, j):
+            return self.strip_copy(row_of(j), p, wc_s, wc_r, j - 1, across_c)
+
+        def by_yc(self, j):
+            return self.strip_copy(row_of(j), p + 2 - 4 * y, wc_s, wc_r, peers - 2 + j, across_c)
+
+        def start(self):
+            loop(1, zs, lambda k: self.by_z(k).start())
+            self.by_x(0).start()
+
+        def after_z(self):
+            def one(k):
+                self.by_z(k).wait_recv()
+                self.by_x(k).start()
+                self.by_y(k).start()
+                self.by_c(k).start()
+            loop(1, zs, one)
+
+        def after_x(self):
+            def one(k):
+                self.by_x(k).wait_recv()
+                self.by_y(zs + k).start()
+                self.by_c(zs + k).start()
+            loop(0, zs, one)
+
+        def after_y(self):
+            def one(j):
+                self.by_y(j).wait_recv()
+                self.by_yc(j).start()
+            loop(1, peers, one)
+
+        def after_c(self):
+            def one(j):
+                self.by_c(j).wait_recv()
+                self.by_yc(j).wait_recv()
+            loop(1, peers, one)
+
+        def sent(self):
+            def one(j):
+                self.by_y(j).wait_send()
+                self.by_c(j).wait_send()
+                self.by_yc(j).wait_send()
+            loop(1, zs, lambda k: self.by_z(k).wait_send())
+            loop(0, zs, lambda k: self.by_x(k).wait_send())
+            loop(1, peers, one)
+
+    near, far = Wave(0), Wave(1)
 
     def slot_copy(k):
         d = lax.rem(r + k, peers)
@@ -231,8 +281,7 @@
 
     feats_copy = remote(fa.at[0], fa.at[1], ff_s, ff_r, across_x)
 
-    loop(1, zs, lambda k: by_z(k).start())
-    by_x(0).start()
+    near.start()
     for copy in loads[:2]:
         copy.wait()
     forward_list = [toh[0, i] for i in range(blocks)]
@@ -244,29 +293,12 @@
     out_buf[...] = dot(place(srow), grad_v[...]).astype(BF16).reshape(peers, per_peer, channels)
     arr_buf[r] = out_buf[r]
 
-    def after_z(k):
-        by_z(k).wait_recv()
-        by_x(k).start()
-        by_y(k).start()
-        by_c(k).start()
-
-    def after_x(k):
-        by_x(k).wait_recv()
-        by_y(zs + k).start()
-        by_c(zs + k).start()
-
-    def after_y(j):
-        by_y(j).wait_recv()
-        by_yc(j).start()
-
-    def after_c(j):
-        by_c(j).wait_recv()
-        by_yc(j).wait_recv()
-
-    loop(1, zs, after_z)
-    loads[5].wait()
+    near.after_z()
+    far.start()
+    loads[4].wait()
     feats_copy.start()
-    loop(0, zs, after_x)
+    near.after_x()
+    far.after_z()
     loop(1, peers, lambda k: slot_copy(k).start())
     feats_copy.wait_recv()
 
@@ -274,14 +306,15 @@
         ft[:, pl.ds(pl.multiple_of(i * rows, rows), rows)] = fa[i].astype(F32).T.astype(BF16)
 
     loop(0, 2, turn)
-    loop(1, peers, after_y)
-    loop(1, peers, after_c)
+    near.after_y()
+    far.after_x()
+    near.after_c()
 
     def pair_cols(hp, base=0):
         return pl.ds(pl.multiple_of(base + hp * PAIR, PAIR), PAIR)
 
     def weight(i, hp):
-        return wf[:, :, :, pair_cols(hp, i * channels)].reshape(shard * peers, PAIR)
+        return wf[lax.div(hp, 2), :, :, :, pair_cols(lax.rem(hp, 2), i * half)].reshape(shard * peers, PAIR)
 
     head_size = channels // HEADS
     scale = head_size ** (-0.5)
@@ -306,7 +339,10 @@
             parts.append(dot(v_t[e * head_size : (e + 1) * head_size], probs.astype(BF16)))
         at_v[cols, :] = jnp.concatenate(parts, axis=0).astype(BF16)
 
-    loop(0, pairs, forward)
+    loop(0, pairs // 2, forward)
+    far.after_y()
+    far.after_c()
+    loop(pairs // 2, pairs, forward)
     loop(1, peers, lambda k: slot_copy(k).wait_recv())
     h_v[...] = contract_rows(place(rrow), arr_buf[...].reshape(slot_rows, channels)).astype(BF16)
     hf_v[...] = jnp.zeros_like(hf_v)
@@ -317,7 +353,7 @@
     def backward(hp):
         cols = pair_cols(hp)
         qp, kp, vp = q_v[:, cols], k_v[:, cols], v_v[:, cols]
-        w_rows = wf[pl.ds(hp * (PAIR // shard), PAIR // shard), :, :, wide:].reshape(PAIR, channels)
+        w_rows = wf[1, pl.ds(hp * (PAIR // shard), PAIR // shard), :, :, wide // 2 :].reshape(PAIR, channels)
         gp = contract_cols(h_v[...], w_rows).astype(BF16)
         k_t = kp.astype(F32).T.astype(BF16)
         dk = dv = None
@@ -443,9 +479,6 @@
     def sent_rows(k):
         slot_copy(k).wait_send()
         back_copy(k).wait_send()
-        by_y(k).wait_send()
-        by_c(k).wait_send()
-        by_yc(k).wait_send()
 
     def sent_chunk(ch):
         dk_copy(ch).wait_send()
@@ -456,8 +489,8 @@
         for k in range(1, 4):
             red5(ch, k).wait_send()
 
-    loop(1, zs, lambda k: by_z(k).wait_send())
-    loop(0, zs, lambda k: by_x(k).wait_send())
+    near.sent()
+    far.sent()
     feats_copy.wait_send()
     loop(1, peers, sent_rows)
     loop(0, pairs, sent_chunk)
@@ -497,9 +530,9 @@
     width = 4 * PAIR
     scratch = [
         vm(rows, channels), vm(share, wide, kind=F32), vm(share, channels, kind=F32), dma((3,)),
-        vm(peers, 4, STRIP, wide + channels),
-        dma((zs - 1,)), dma((zs - 1,)), dma((zs,)), dma((zs,)),
-        dma((peers - 1,)), dma((peers - 1,)), dma((2 * peers - 2,)), dma((2 * peers - 2,)),
+        vm(2, peers, 4, STRIP, wide // 2 + channels),
+        dma((2, zs - 1)), dma((2, zs - 1)), dma((2, zs)), dma((2, zs)),
+        dma((2, peers - 1)), dma((2, peers - 1)), dma((2, 2 * peers - 2)), dma((2, 2 * peers - 2)),
         vm(peers, slot_rows // peers, channels), vm(peers, slot_rows // peers, channels),
         dma((peers - 1,)), dma((peers - 1,)),
         vm(peers, slot_rows // peers, channels), vm(peers, slot_rows // peers, channels),
@@ -510,7 +543,7 @@
         vm(2 * rows, channels), vm(2 * rows, channels), vm(rows, channels, kind=F32),
         vm(pairs, 2, rows, PAIR), vm(pairs, 2, rows, PAIR), dma((pairs,)), dma((pairs,)),
         dma((pairs, zs + 5)), dma((pairs, zs + 5)),
-        vm(rows, channels), pltpu.SMEM((1, blocks), jnp.int32), pltpu.SMEM((1, blocks), jnp.int32), dma((6,)),
+        vm(rows, channels), pltpu.SMEM((1, blocks), jnp.int32), pltpu.SMEM((1, blocks), jnp.int32), dma((11,)),
         vm(HEADS, 2 * rows, rows, kind=F32),
         vm(pairs, 2, 2, 2, zs, STRIP, width), vm(pairs, 2, 2, zs, STRIP, width), vm(pairs, 2, 2, zs, STRIP, width),
         vm(pairs, 2, zs, STRIP, width), vm(pairs, 2, zs, STRIP, width),

time: 75.1 us -> 76.4 us (1.017)
  Pallas kernels: 74.3 us -> 75.6 us
    pallas_call x1, Pallas kernels: 72.4 us -> 73.7 us  [per_device(): pl.pallas_call(body, out_shape=shapes, in_specs=[hbm] * 6, out_specs=(hbm...]
where the time goes in v6:
time: 76.4 us; the launch traced here: 76.3 us
  Pallas kernels  75.6 us (99%)
    pallas_call x1, Pallas kernels, per_device(): pl.pallas_call(body, out_shape=shapes, in_specs=[hbm] * 6, out_specs=(hbm...  73.7 us
    pallas_call x1, Pallas kernels, per_device(): pl.pallas_call(hand_over, out_shape=shapes, in_specs=[hbm] * 3, out_specs...  1.91 us

profile of v6, /device:TPU:0, one launch (start us, length us, event | category | flops | bytes accessed | tf_op | source)
XLA Modules:
  0.0 76.3 jit_solution(5788978375319660225)
XLA Ops:
  0.6 73.7 %shard_map.85 = (bf16[256,512]{1,0:T(8,128)(2,1)}, f32[64,1536]{1,0:T(8,128)}, f32[64,512]{1,0:T(8,128)}) custom-call(bf16[256,512]{1,0:T(8,128)(2,1)} %bitcast.5, bf16[256,512]{1,0:T(8,128)(2,1)} %bitcast.6, bf16[4,16,1536]{2,1,0:T(8,128)(2,1)} %bitcast.7, bf16[4,16,512]{2,1,0:T(8,128)(2,1)} %bitcast.8, s32[1,8]{1,0:T(1,128)} %refs_4_.1, s32[1,8]{1,0:T(1,128)} %refs_5_.1), custom_call_target="tpu_custom_call" | custom-call | tf_op jit(solution)/shard_map/pallas_call | solution.py:563
  74.3 1.9 %shard_map.86 = (bf16[256,512]{1,0:T(8,128)(2,1)}, f32[64,1536]{1,0:T(8,128)}, f32[64,512]{1,0:T(8,128)}) custom-call(bf16[256,512]{1,0:T(8,128)(2,1)} %get-tuple-element.9.refs_0_, f32[64,1536]{1,0:T(8,128)} %get-tuple-element.10.refs_1_, f32[64,512]{1,0:T(8,128)} %get-tuple-element.11.refs_2_), custom_call_target="tpu_custom_call" | custom-call | tf_op jit(solution)/shard_map/pallas_call | solution.py:573
